TPU v7x, 32 devices: a whole 2x2x4 slice. The times are simulated.
32 devices in a mesh: section: 4 (over y, core), dp: 8 (over z, x).
Axes of the slice: x: 2, y: 2, z: 4, core: 2. Of those that a mesh axis runs over, the one named last changes fastest.
Arguments:
- inputs: bfloat16 [1280, 2560], P('dp'), may hold values from -6 to 6
- cotangent: bfloat16 [1280, 2560], P('dp'), may hold values from -6 to 6
- weights: bfloat16 [4, 2560, 2560], P('section', 'dp'), may hold values from -0.0625 to 0.0625
- lengths: int32 [40], P('dp'), may hold values from 1 to 32, as said below
Outputs:
- pre_inputs: bfloat16 [4, 1280, 2560], P('section', 'dp')
- pre_grads: bfloat16 [4, 1280, 2560], P('section', 'dp')
Inputs may be any that keep to these rules, and one draw needn't show every extreme that they name: `lengths`: each micro-batch has at least one live token; some micro-batch is full and some has exactly one.
All inputs are finite; a program needn't handle non-finite values.
Results may differ from a plain program's by a relative error of at most 0.012.
Values may be sent and summed in bfloat16 or wider, within the bound.
A program may use at most 64 MiB of HBM per device.

v0:
```python
import jax
import jax.numpy as jnp
from jax import lax
from jax.sharding import PartitionSpec as P

BLOCK = 160


epsilon = 1e-05
damping = 0.1


def from_behind(array, axis, by):
    count = lax.axis_size(axis)
    pairs = [(i, i + by) for i in range(count) if 0 <= i + by < count]
    return lax.ppermute(array, axis, pairs)


def normalize(hidden):
    wide = hidden.astype(jnp.float32)
    factor = lax.rsqrt(jnp.mean(wide * wide, axis=-1, keepdims=True) + epsilon)
    return (wide * factor, factor)


def invert_blocks(blocks, counted):
    order = blocks.shape[-1]
    identity = jnp.eye(order, dtype=jnp.float32)
    damped = blocks / counted + damping * identity
    lower = jnp.linalg.cholesky(damped)
    half_way = lax.linalg.triangular_solve(
        lower, jnp.broadcast_to(identity, damped.shape), left_side=True, lower=True
    )
    inverse = lax.linalg.triangular_solve(
        lower, half_way, left_side=True, lower=True, transpose_a=True
    )
    return inverse.astype(jnp.bfloat16)


def apply_blocks(values, inverse):
    shaped = values.reshape(values.shape[0], inverse.shape[0], inverse.shape[1])
    result = jnp.einsum("tbi,bij->tbj", shaped, inverse, preferred_element_type=jnp.float32)
    return result.reshape(1, values.shape[0], values.shape[1]).astype(jnp.bfloat16)


def on_device(inputs, cotangent, weights, lengths):
    section_index = lax.axis_index("section")
    section_count = lax.axis_size("section")
    token_count, width = inputs.shape
    micro_count = lengths.shape[0]
    batch_rows = token_count // micro_count
    moments = micro_count + section_count - 1
    full_weight = lax.all_gather(weights, "dp", axis=1, tiled=True)[0]
    empty = jnp.zeros((batch_rows, width), jnp.bfloat16)
    stored = jnp.zeros((micro_count, batch_rows, width), jnp.bfloat16)

    def forward_moment(moment, carry):
        outgoing, hidden_store = carry
        arrived = from_behind(outgoing, "section", 1)
        position = moment - section_index
        active = jnp.logical_and(position >= 0, position < micro_count)
        picked = jnp.clip(position, 0, micro_count - 1)
        fresh = lax.dynamic_slice_in_dim(inputs, picked * batch_rows, batch_rows, 0)
        current = jnp.where(section_index == 0, fresh, arrived)

        def advance(operands):
            state, kept = operands
            normed, unused = normalize(state)
            activation = normed.astype(jnp.bfloat16)
            result = (
                state.astype(jnp.float32)
                + jnp.dot(activation, full_weight, preferred_element_type=jnp.float32)
            ).astype(jnp.bfloat16)
            return (result, lax.dynamic_update_index_in_dim(kept, state, picked, 0))

        def forward_resting(operands):
            return (jnp.zeros_like(operands[0]), operands[1])

        return lax.cond(active, advance, forward_resting, (current, hidden_store))

    unused_out, hidden_store = lax.fori_loop(0, moments, forward_moment, (empty, stored))

    def backward_moment(moment, carry):
        outgoing, grad_store = carry
        arrived = from_behind(outgoing, "section", -1)
        position = moment - (section_count - 1 - section_index)
        active = jnp.logical_and(position >= 0, position < micro_count)
        picked = jnp.clip(position, 0, micro_count - 1)
        fresh = lax.dynamic_slice_in_dim(cotangent, picked * batch_rows, batch_rows, 0)
        current = jnp.where(section_index == section_count - 1, fresh, arrived)

        def retreat(operands):
            state, kept = operands
            hidden = lax.dynamic_index_in_dim(hidden_store, picked, 0, keepdims=False)
            normed, factor = normalize(hidden)
            back = lax.dot_general(
                state, full_weight, (((1,), (1,)), ((), ())), preferred_element_type=jnp.float32
            )
            through = factor * (back - normed * jnp.mean(back * normed, axis=-1, keepdims=True))
            result = (state.astype(jnp.float32) + through).astype(jnp.bfloat16)
            return (result, lax.dynamic_update_index_in_dim(kept, state, picked, 0))

        def backward_resting(operands):
            return (jnp.zeros_like(operands[0]), operands[1])

        return lax.cond(active, retreat, backward_resting, (current, grad_store))

    unused_back, grad_store = lax.fori_loop(0, moments, backward_moment, (empty, stored))
    activations = normalize(hidden_store.reshape(token_count, width))[0].astype(jnp.bfloat16)
    gradients = grad_store.reshape(token_count, width)
    live = (jnp.arange(batch_rows)[None, :] < lengths[:, None]).reshape(token_count, 1)
    counted = lax.psum(jnp.sum(live.astype(jnp.float32)), "dp")
    blocks_each = width // BLOCK
    zero_value = jnp.zeros((), jnp.bfloat16)
    masked_act = jnp.where(live, activations, zero_value).reshape(token_count, blocks_each, BLOCK)
    masked_grad = jnp.where(live, gradients, zero_value).reshape(token_count, blocks_each, BLOCK)
    gram_act = jnp.einsum(
        "tbi,tbj->bij", masked_act, masked_act, preferred_element_type=jnp.float32
    )
    gram_grad = jnp.einsum(
        "tbi,tbj->bij", masked_grad, masked_grad, preferred_element_type=jnp.float32
    )
    stacked = jnp.concatenate([gram_act, gram_grad], axis=0)
    owned = lax.psum_scatter(stacked, "dp", scatter_dimension=0, tiled=True)
    inverses = lax.all_gather(invert_blocks(owned, counted), "dp", axis=0, tiled=True)
    pre_inputs = apply_blocks(activations, inverses[:blocks_each])
    pre_grads = apply_blocks(gradients, inverses[blocks_each:])
    return (pre_inputs, pre_grads)


def solution(mesh):
    in_specs = (P("dp", None), P("dp", None), P("section", "dp", None), P("dp"))
    out_specs = (P("section", "dp", None), P("section", "dp", None))
    return jax.shard_map(
        on_device, mesh=mesh, in_specs=in_specs, out_specs=out_specs, check_vma=False
    )
```

profile of v0, /device:TPU:0, one launch (start us, length us, event | category | flops | bytes accessed | tf_op | source)
XLA Modules:
  0.0 836.1 jit_solution(5354860686367160503)
XLA Ops:
  8.8 187.0 %all-gather.3.cloned.1.call-done = bf16[1,2560,2560]{2,1,0:T(8,128)(2,1)} async-done(((bf16[1,320,2560]{2,1,0:T(8,128)(2,1)}), bf16[1,2560,2560]{2,1,0:T(8,128)(2,1)}) %all-gather.3.cloned.1.call-update) | async-done | bytes 13107216 | tf_op jit(solution)/shard_map/all_gather | solution.py:52
  196.5 95.3 %while.41 = (s32[]{:T(128)}, bf16[32,2560]{1,0:T(8,128)(2,1)}, bf16[5,32,2560]{2,1,0:T(8,128)(2,1)S(1)}, s32[]{:T(128)}, pred[]{:T(512)}, /*index=5*/bf16[160,25...) while((s32[]{:T(128)}, bf16[32,2560]{1,0:T(8,128)(2,1)}, ...), condition=%wide.region_4.5_spmd, body=%wide.region_0.4_spmd.sunk | while | flops 420249632 | bytes 14910282 | solution.py:80
  199.1 8.9 %conditional.4 = (bf16[32,2560]{1,0:T(8,128)(2,1)}, bf16[5,32,2560]{2,1,0:T(8,128)(2,1)S(1)}) conditional(s32[]{:T(128)} %convert_element_type.158, bf16[5,32,2560]{2,1,0:T(8,128)(2,1)S(1)} %get-tuple-element.716, (pred[]{:T(512)}, s32[]{:T(128)}, bf16[160,2560]{1,0:T(8,128)(2,1)}, bf16[32,2560]{1,0:T(8,128)(2,1)S(1)}, bf16[2560,2560]{1,0:T(8,128)(2,1)}, ...), branch_computations={%region_1.1_spmd, %region_2.3_spmd} | conditional | flops 420249632 | bytes 14254687 | solution.py:78
  210.5 8.9 %conditional.4 = (bf16[32,2560]{1,0:T(8,128)(2,1)}, bf16[5,32,2560]{2,1,0:T(8,128)(2,1)S(1)}) conditional(s32[]{:T(128)} %convert_element_type.158, bf16[5,32,2560]{2,1,0:T(8,128)(2,1)S(1)} %get-tuple-element.716, (pred[]{:T(512)}, s32[]{:T(128)}, bf16[160,2560]{1,0:T(8,128)(2,1)}, bf16[32,2560]{1,0:T(8,128)(2,1)S(1)}, bf16[2560,2560]{1,0:T(8,128)(2,1)}, ...), branch_computations={%region_1.1_spmd, %region_2.3_spmd} | conditional | flops 420249632 | bytes 14254687 | solution.py:78
  222.9 8.9 %conditional.4 = (bf16[32,2560]{1,0:T(8,128)(2,1)}, bf16[5,32,2560]{2,1,0:T(8,128)(2,1)S(1)}) conditional(s32[]{:T(128)} %convert_element_type.158, bf16[5,32,2560]{2,1,0:T(8,128)(2,1)S(1)} %get-tuple-element.716, (pred[]{:T(512)}, s32[]{:T(128)}, bf16[160,2560]{1,0:T(8,128)(2,1)}, bf16[32,2560]{1,0:T(8,128)(2,1)S(1)}, bf16[2560,2560]{1,0:T(8,128)(2,1)}, ...), branch_computations={%region_1.1_spmd, %region_2.3_spmd} | conditional | flops 420249632 | bytes 14254687 | solution.py:78
  236.3 8.9 %conditional.4 = (bf16[32,2560]{1,0:T(8,128)(2,1)}, bf16[5,32,2560]{2,1,0:T(8,128)(2,1)S(1)}) conditional(s32[]{:T(128)} %convert_element_type.158, bf16[5,32,2560]{2,1,0:T(8,128)(2,1)S(1)} %get-tuple-element.716, (pred[]{:T(512)}, s32[]{:T(128)}, bf16[160,2560]{1,0:T(8,128)(2,1)}, bf16[32,2560]{1,0:T(8,128)(2,1)S(1)}, bf16[2560,2560]{1,0:T(8,128)(2,1)}, ...), branch_computations={%region_1.1_spmd, %region_2.3_spmd} | conditional | flops 420249632 | bytes 14254687 | solution.py:78
  252.1 8.9 %conditional.4 = (bf16[32,2560]{1,0:T(8,128)(2,1)}, bf16[5,32,2560]{2,1,0:T(8,128)(2,1)S(1)}) conditional(s32[]{:T(128)} %convert_element_type.158, bf16[5,32,2560]{2,1,0:T(8,128)(2,1)S(1)} %get-tuple-element.716, (pred[]{:T(512)}, s32[]{:T(128)}, bf16[160,2560]{1,0:T(8,128)(2,1)}, bf16[32,2560]{1,0:T(8,128)(2,1)S(1)}, bf16[2560,2560]{1,0:T(8,128)(2,1)}, ...), branch_computations={%region_1.1_spmd, %region_2.3_spmd} | conditional | flops 420249632 | bytes 14254687 | solution.py:78
  268.5 13.9 %collective-permute-start = (bf16[32,2560]{1,0:T(8,128)(2,1)}, bf16[32,2560]{1,0:T(8,128)(2,1)S(1)}, u32[]{:S(2)}, u32[]{:S(2)}) collective-permute-start(bf16[32,2560]{1,0:T(8,128)(2,1)} %get-tuple-element.715), channel_id=1, source_target_pairs={{0,8},{8,16},{16,24},{1,9},{9,17},{17,25},{2,10},{10,18},{18,26},{... | collective-permute-start | bytes 491528 | tf_op jit(solution)/shard_map/while/body/eval_jaxpr/ppermute | solution.py:16
  295.2 151.9 %while.42 = (s32[]{:T(128)}, bf16[32,2560]{1,0:T(8,128)(2,1)}, bf16[5,32,2560]{2,1,0:T(8,128)(2,1)}, s32[]{:T(128)}, pred[]{:T(512)}, /*index=5*/bf16[160,2560]{...) while((s32[]{:T(128)}, bf16[32,2560]{1,0:T(8,128)(2,1)}, ...), condition=%wide.region_11.12_spmd, body=%wide.region_6.11_spmd.sunk | while | flops 420741152 | bytes 16058341 | solution.py:107
  296.5 13.8 %collective-permute-done.1 = bf16[32,2560]{1,0:T(8,128)(2,1)} collective-permute-done((bf16[32,2560]{1,0:T(8,128)(2,1)}, bf16[32,2560]{1,0:T(8,128)(2,1)}, u32[]{:S(2)}, u32[]{:S(2)}) %collective-permute-start.1) | collective-permute-done | bytes 163872 | tf_op jit(solution)/shard_map/while/body/eval_jaxpr/ppermute | solution.py:16
  328.6 33.5 %collective-permute-done.1 = bf16[32,2560]{1,0:T(8,128)(2,1)} collective-permute-done((bf16[32,2560]{1,0:T(8,128)(2,1)}, bf16[32,2560]{1,0:T(8,128)(2,1)}, u32[]{:S(2)}, u32[]{:S(2)}) %collective-permute-start.1) | collective-permute-done | bytes 163872 | tf_op jit(solution)/shard_map/while/body/eval_jaxpr/ppermute | solution.py:16
  362.2 11.4 %conditional.5 = (bf16[32,2560]{1,0:T(8,128)(2,1)}, bf16[5,32,2560]{2,1,0:T(8,128)(2,1)}) conditional(s32[]{:T(128)} %convert_element_type.159, bf16[5,32,2560]{2,1,0:T(8,128)(2,1)} %get-tuple-element.747, (pred[]{:T(512)}, s32[]{:T(128)}, bf16[160,2560]{1,0:T(8,128)(2,1)}, bf16[32,2560]{1,0:T(8,128)(2,1)}, bf16[5,32,2560]{2,1,0:T(8,128)(2,1)S(1)}, ...), branch_computations={%region_7.7_spmd, %region_8.10_spmd} | conditional | flops 420741152 | bytes 15402730 | solution.py:105
  364.1 8.7 %fusion.7 = (f32[32]{0:T(128)S(1)}, f32[32,2560]{1,0:T(8,128)S(1)}) fusion(f32[32]{0:T(128)S(1)} %add_rsqrt_fusion.1, bf16[5,32,2560]{2,1,0:T(8,128)(2,1)S(1)} %get-tuple-element.504, s32[]{:T(128)S(6)} %min.21, bf16[32,2560]{1,0:T(8,128)(2,1)S(1)} %get-tuple-element.583, bf16[2560,2560]{1,0:T(8,128)(2,1)} %get-tuple-element.505), kind=kOutput, calls=%fused_computation.14 | convolution fusion | flops 419758048 | bytes 13762820 | tf_op jit(solution)/shard_map/while/body/eval_jaxpr/cond/branch_1_fun/dot_general | solution.py:95
  380.6 11.4 %conditional.5 = (bf16[32,2560]{1,0:T(8,128)(2,1)}, bf16[5,32,2560]{2,1,0:T(8,128)(2,1)}) conditional(s32[]{:T(128)} %convert_element_type.159, bf16[5,32,2560]{2,1,0:T(8,128)(2,1)} %get-tuple-element.747, (pred[]{:T(512)}, s32[]{:T(128)}, bf16[160,2560]{1,0:T(8,128)(2,1)}, bf16[32,2560]{1,0:T(8,128)(2,1)}, bf16[5,32,2560]{2,1,0:T(8,128)(2,1)S(1)}, ...), branch_computations={%region_7.7_spmd, %region_8.10_spmd} | conditional | flops 420741152 | bytes 15402730 | solution.py:105
  399.0 11.4 %conditional.5 = (bf16[32,2560]{1,0:T(8,128)(2,1)}, bf16[5,32,2560]{2,1,0:T(8,128)(2,1)}) conditional(s32[]{:T(128)} %convert_element_type.159, bf16[5,32,2560]{2,1,0:T(8,128)(2,1)} %get-tuple-element.747, (pred[]{:T(512)}, s32[]{:T(128)}, bf16[160,2560]{1,0:T(8,128)(2,1)}, bf16[32,2560]{1,0:T(8,128)(2,1)}, bf16[5,32,2560]{2,1,0:T(8,128)(2,1)S(1)}, ...), branch_computations={%region_7.7_spmd, %region_8.10_spmd} | conditional | flops 420741152 | bytes 15402730 | solution.py:105
  417.3 11.4 %conditional.5 = (bf16[32,2560]{1,0:T(8,128)(2,1)}, bf16[5,32,2560]{2,1,0:T(8,128)(2,1)}) conditional(s32[]{:T(128)} %convert_element_type.159, bf16[5,32,2560]{2,1,0:T(8,128)(2,1)} %get-tuple-element.747, (pred[]{:T(512)}, s32[]{:T(128)}, bf16[160,2560]{1,0:T(8,128)(2,1)}, bf16[32,2560]{1,0:T(8,128)(2,1)}, bf16[5,32,2560]{2,1,0:T(8,128)(2,1)S(1)}, ...), branch_computations={%region_7.7_spmd, %region_8.10_spmd} | conditional | flops 420741152 | bytes 15402730 | solution.py:105
  435.7 11.4 %conditional.5 = (bf16[32,2560]{1,0:T(8,128)(2,1)}, bf16[5,32,2560]{2,1,0:T(8,128)(2,1)}) conditional(s32[]{:T(128)} %convert_element_type.159, bf16[5,32,2560]{2,1,0:T(8,128)(2,1)} %get-tuple-element.747, (pred[]{:T(512)}, s32[]{:T(128)}, bf16[160,2560]{1,0:T(8,128)(2,1)}, bf16[32,2560]{1,0:T(8,128)(2,1)}, bf16[5,32,2560]{2,1,0:T(8,128)(2,1)S(1)}, ...), branch_computations={%region_7.7_spmd, %region_8.10_spmd} | conditional | flops 420741152 | bytes 15402730 | solution.py:105
  460.7 21.0 %psum.7 = f32[]{:T(128)} all-reduce(f32[]{:T(128)} %convert_reduce_fusion), channel_id=1, replica_groups=mesh['section'=4,'dp'=8] {'dp'}, use_global_device_ids=true, to_apply=%region_14.15 | all-reduce | flops 1 | bytes 8 | tf_op jit(solution)/shard_map/psum | solution.py:111
  485.6 74.3 %reduce-scatter.2.cloned.1.call-done = f32[4,160,160]{1,2,0:T(8,128)} async-done(((f32[32,160,160]{1,2,0:T(8,128)}), f32[4,160,160]{1,2,0:T(8,128)}) %reduce-scatter.2.cloned.1.call-update) | async-done | bytes 409616 | tf_op jit(solution)/shard_map/reduce_scatter | solution.py:123
  567.6 46.9 %custom-call.18 = f32[4,128,128]{2,1,0:T(8,128)S(1)} custom-call(f32[4,128,128]{2,1,0:T(8,128)S(1)} %cholesky.129), custom_call_target="Cholesky" | custom-call | tf_op jit(solution)/shard_map/jit(cholesky)/cholesky | solution.py:29
  616.6 40.8 %custom-call.19 = f32[4,1,128,128]{2,3,1,0:T(8,128)} custom-call(f32[4,1,128,128]{3,2,1,0:T(8,128)} %get-tuple-element.587), custom_call_target="InvertDiagBlocksLowerTriangular" | custom-call | tf_op jit(solution)/shard_map/jit(cholesky)/cholesky | solution.py:29
  659.8 11.7 %custom-call.20 = f32[4,32,32]{2,1,0:T(8,128)S(1)} custom-call(f32[4,32,32]{2,1,0:T(8,128)S(1)} %convolution_subtract_fusion.2), custom_call_target="Cholesky" | custom-call | tf_op jit(solution)/shard_map/jit(cholesky)/cholesky | solution.py:29
  676.8 79.6 %custom-call.21 = f32[4,2,128,128]{2,3,1,0:T(8,128)S(1)} custom-call(f32[4,2,128,128]{3,2,1,0:T(8,128)} %pad_maximum_fusion.1), custom_call_target="InvertDiagBlocksLowerTriangular" | custom-call | tf_op jit(solution)/shard_map/triangular_solve | solution.py:33
  764.7 54.6 %all-gather.5.cloned.1.call-done = bf16[32,160,160]{2,1,0:T(8,128)(2,1)} async-done(((bf16[4,160,160]{2,1,0:T(8,128)(2,1)}), bf16[32,160,160]{2,1,0:T(8,128)(2,1)}) %all-gather.5.cloned.1.call-update) | async-done | bytes 1638416 | tf_op jit(solution)/shard_map/all_gather | solution.py:124
  (167 shorter events, 240.0 us)
Async XLA Ops:
  7.2 188.6 %all-gather.3.cloned.1.call-start = ((), (), s32[]{:S(2)}) async-start(), calls=%async_computation.1 | async-start | bytes 14745600 | tf_op jit(solution)/shard_map/all_gather | solution.py:52
  7.9 552.0 %reduce-scatter.2.cloned.1.call-start = ((), (), s32[]{:S(2)}) async-start(), calls=%async_computation.2 | async-start | bytes 5898240 | tf_op jit(solution)/shard_map/reduce_scatter | solution.py:123
  196.5 2.6 collective-permute-start
  208.0 2.5 collective-permute-start
  219.4 3.5 collective-permute-start
  231.8 4.5 collective-permute-start
  245.3 6.8 collective-permute-start
  261.0 6.8 collective-permute-start
  268.5 15.1 %collective-permute-start = (bf16[32,2560]{1,0:T(8,128)(2,1)}, bf16[32,2560]{1,0:T(8,128)(2,1)S(1)}, u32[]{:S(2)}, u32[]{:S(2)}) collective-permute-start(bf16[32,2560]{1,0:T(8,128)(2,1)} %get-tuple-element.715), channel_id=1, source_target_pairs={{0,8},{8,16},{16,24},{1,9},{9,17},{17,25},{2,10},{10,18},{18,26},{... | collective-permute-start | bytes 491528 | tf_op jit(solution)/shard_map/while/body/eval_jaxpr/ppermute | solution.py:16
  284.3 6.8 collective-permute-start
  295.2 15.1 %collective-permute-start.1 = (bf16[32,2560]{1,0:T(8,128)(2,1)}, bf16[32,2560]{1,0:T(8,128)(2,1)}, u32[]{:S(2)}, u32[]{:S(2)}) collective-permute-start(bf16[32,2560]{1,0:T(8,128)(2,1)} %get-tuple-element.746), channel_id=1, source_target_pairs={{8,0},{16,8},{24,16},{9,1},{17,9},{25,17},{10,2},{18,10},{26,18},{... | collective-permute-start | bytes 491528 | tf_op jit(solution)/shard_map/while/body/eval_jaxpr/ppermute | solution.py:16
  311.0 7.6 collective-permute-start.1
  319.3 7.4 collective-permute-start.1
  327.3 34.9 %collective-permute-start.1 = (bf16[32,2560]{1,0:T(8,128)(2,1)}, bf16[32,2560]{1,0:T(8,128)(2,1)}, u32[]{:S(2)}, u32[]{:S(2)}) collective-permute-start(bf16[32,2560]{1,0:T(8,128)(2,1)} %get-tuple-element.746), channel_id=1, source_target_pairs={{8,0},{16,8},{24,16},{9,1},{17,9},{25,17},{10,2},{18,10},{26,18},{... | collective-permute-start | bytes 491528 | tf_op jit(solution)/shard_map/while/body/eval_jaxpr/ppermute | solution.py:16
  373.6 6.9 collective-permute-start.1
  392.0 6.9 collective-permute-start.1
  410.4 6.9 collective-permute-start.1
  428.8 6.9 collective-permute-start.1
  450.7 6.0 copy-start.4
  459.4 359.9 %all-gather.5.cloned.1.call-start = ((), (), s32[]{:S(2)}) async-start(), calls=%async_computation.3 | async-start | bytes 2949120 | tf_op jit(solution)/shard_map/all_gather | solution.py:124
  559.9 5.0 copy-start
  566.7 0.8 copy-start.2
  616.6 139.8 %slice-start = ((f32[160,160]{0,1:T(8,128)}), f32[128,160]{0,1:T(8,128)S(1)}, s32[]{:S(2)}) async-start(f32[160,160]{0,1:T(8,128)} %copy-done.3), calls=%async_computation.4 | async-start | bytes 163840 | tf_op jit(solution)/shard_map/triangular_solve | solution.py:30
  756.8 62.5 %copy-start.5 = (f32[160]{0:T(256)S(1)}, f32[160]{0:T(256)}, u32[]{:S(2)}) copy-start(f32[160]{0:T(256)} %copy-done.4) | copy-start | bytes 1924
  (3 other events, 2.2 us)
Sparse Core Ops, SparseCore 0:
  10.2 185.5 all-gather.2
  459.5 100.3 reduce-scatter.1
  764.8 54.3 all-gather.4
where the time goes:
time: 838 us; the launch traced here: 836 us
  waiting for transfers between devices  408 us (49%)
  other arithmetic  216 us (26%)
  matrix products  103 us (12%)
  starting transfers between devices  49.2 us (6%)
  local copies, waits for them, and re-layouts  23.7 us (3%)
  blocking collectives  21 us (3%)
  between operations  13.9 us (2%)
    all_gather x1, waiting for transfers between devices, on_device(): full_weight = lax.all_gather(weights, 'dp', axis=1, tiled=True)[0]  187 us
    another operation x10, other arithmetic, invert_blocks(): lower = jnp.linalg.cholesky(damped)  104 us
    ppermute x16, waiting for transfers between devices, from_behind(): return lax.ppermute(array, axis, pairs)  91.9 us
    another operation x8, other arithmetic, invert_blocks(): lax.linalg.triangular_solve(lower, half_way, left_side=True, lower=True,...  83.8 us
    reduce_scatter x1, waiting for transfers between devices, on_device(): owned = lax.psum_scatter(stacked, 'dp', scatter_dimension=0, tiled=True)  74.3 us
    all_gather x1, waiting for transfers between devices, on_device(): lax.all_gather(invert_blocks(owned, counted), 'dp', axis=0, tiled=True)  54.6 us
    ppermute x16, starting transfers between devices, from_behind(): return lax.ppermute(array, axis, pairs)  49.1 us
    dot_general x5, matrix products, retreat(): lax.dot_general(state, full_weight, (((1,), (1,)), ((), ())), preferred_e...  43.6 us
  transfers between devices with their start and end apart: 19, of which 19 were waited for; matrix products, arithmetic and copies ran while one was open for 1% of the time, Pallas kernels for 0%

commit v1 on v0

v1 whole, which is shorter than its diff:
```python
import functools

import jax
import jax.numpy as jnp
from jax import lax
from jax.experimental import pallas as pl
from jax.experimental.pallas import tpu as pltpu
from jax.sharding import PartitionSpec as P

BLOCK = 160
PANEL = 32
LANES = 128
PACK = LANES // PANEL

epsilon = 1e-05
damping = 0.1

exact_dot = functools.partial(
    lax.dot_general, precision=lax.Precision.HIGHEST, preferred_element_type=jnp.float32
)


def normalize(hidden):
    wide = hidden.astype(jnp.float32)
    factor = lax.rsqrt(jnp.mean(wide * wide, axis=-1, keepdims=True) + epsilon)
    return (wide * factor, factor)


def sweep_panel(panel, width):
    rows = lax.broadcasted_iota(jnp.int32, (PANEL, width), 0)
    lanes = lax.broadcasted_iota(jnp.int32, (PANEL, width), 1)
    within = lanes % PANEL
    base = lanes - within
    for k in range(PANEL):
        column = jnp.take_along_axis(panel, base + k, axis=1)
        row = jnp.broadcast_to(panel[k : k + 1, :], (PANEL, width))
        pivot = jnp.broadcast_to(column[k : k + 1, :], (PANEL, width))
        inverse = 1.0 / pivot
        scaled = row * inverse
        inner = panel - column * scaled
        inner = jnp.where(within == k, column * inverse, inner)
        edge = jnp.where(within == k, -inverse, scaled)
        panel = jnp.where(rows == k, edge, inner)
    return panel


def invert_in_place(work, packed, count):
    for start in range(0, count, PACK):
        members = range(start, min(count, start + PACK))
        for k in range(BLOCK // PANEL):
            at = slice(k * PANEL, (k + 1) * PANEL)
            packed[...] = jnp.zeros_like(packed)
            for m in members:
                packed[:, (m - start) * PANEL : (m - start + 1) * PANEL] = work[m, at, at]
            packed[...] = sweep_panel(packed[...], LANES)
            for m in members:
                inverse = -packed[:, (m - start) * PANEL : (m - start + 1) * PANEL]
                row = work[m, at, :]
                across = exact_dot(inverse, row, (((1,), (0,)), ((), ())))
                down = exact_dot(row, inverse, (((0,), (0,)), ((), ())))
                work[m] = work[m] - exact_dot(row, across, (((0,), (0,)), ((), ())))
                work[m, at, :] = across
                work[m, :, at] = down
                work[m, at, at] = -inverse


def invert_kernel(count, counted_ref, blocks_ref, out_ref, work, packed):
    scale = 1.0 / counted_ref[0, 0]
    diagonal = lax.broadcasted_iota(jnp.int32, (BLOCK, BLOCK), 0) == lax.broadcasted_iota(
        jnp.int32, (BLOCK, BLOCK), 1
    )
    for m in range(count):
        work[m] = blocks_ref[m] * scale + jnp.where(diagonal, damping, 0.0)
    invert_in_place(work, packed, count)
    for m in range(count):
        out_ref[m] = (-work[m]).astype(jnp.bfloat16)


def invert_blocks(blocks, counted):
    count = blocks.shape[0]
    return pl.pallas_call(
        functools.partial(invert_kernel, count),
        out_shape=jax.ShapeDtypeStruct(blocks.shape, jnp.bfloat16),
        in_specs=[
            pl.BlockSpec(memory_space=pltpu.SMEM),
            pl.BlockSpec(memory_space=pltpu.VMEM),
        ],
        out_specs=pl.BlockSpec(memory_space=pltpu.VMEM),
        scratch_shapes=[
            pltpu.VMEM(blocks.shape, jnp.float32),
            pltpu.VMEM((PANEL, LANES), jnp.float32),
        ],
        compiler_params=pltpu.CompilerParams(vmem_limit_bytes=32 * 1024 * 1024),
    )(counted.reshape(1, 1), blocks)


def apply_blocks(values, inverse):
    shaped = values.reshape(values.shape[0], inverse.shape[0], inverse.shape[1])
    result = jnp.einsum("tbi,bij->tbj", shaped, inverse, preferred_element_type=jnp.float32)
    return result.reshape(1, values.shape[0], values.shape[1]).astype(jnp.bfloat16)


def on_device(inputs, cotangent, weights, lengths):
    section_index = lax.axis_index("section")
    section_count = lax.axis_size("section")
    token_count, width = inputs.shape
    micro_count = lengths.shape[0]
    batch_rows = token_count // micro_count
    live = (jnp.arange(batch_rows)[None, :] < lengths[:, None]).reshape(token_count, 1)
    counted = lax.psum(jnp.sum(live.astype(jnp.float32)), "dp")
    full_weight = lax.all_gather(weights, "dp", axis=1, tiled=True)[0]

    hidden = inputs
    for stage in range(section_count - 1):
        activation = normalize(hidden)[0].astype(jnp.bfloat16)
        result = (
            hidden.astype(jnp.float32)
            + jnp.dot(activation, full_weight, preferred_element_type=jnp.float32)
        ).astype(jnp.bfloat16)
        arrived = lax.ppermute(result, "section", [(stage, stage + 1)])
        hidden = jnp.where(section_index == stage + 1, arrived, hidden)

    normed, factor = normalize(hidden)
    activations = normed.astype(jnp.bfloat16)
    gradients = cotangent
    for stage in range(section_count - 1, 0, -1):
        back = lax.dot_general(
            gradients, full_weight, (((1,), (1,)), ((), ())), preferred_element_type=jnp.float32
        )
        through = factor * (back - normed * jnp.mean(back * normed, axis=-1, keepdims=True))
        result = (gradients.astype(jnp.float32) + through).astype(jnp.bfloat16)
        arrived = lax.ppermute(result, "section", [(stage, stage - 1)])
        gradients = jnp.where(section_index == stage - 1, arrived, gradients)

    blocks_each = width // BLOCK
    zero_value = jnp.zeros((), jnp.bfloat16)
    masked_act = jnp.where(live, activations, zero_value).reshape(token_count, blocks_each, BLOCK)
    masked_grad = jnp.where(live, gradients, zero_value).reshape(token_count, blocks_each, BLOCK)
    gram_act = jnp.einsum(
        "tbi,tbj->bij", masked_act, masked_act, preferred_element_type=jnp.float32
    )
    gram_grad = jnp.einsum(
        "tbi,tbj->bij", masked_grad, masked_grad, preferred_element_type=jnp.float32
    )
    stacked = jnp.concatenate([gram_act, gram_grad], axis=0)
    owned = lax.psum_scatter(stacked, "dp", scatter_dimension=0, tiled=True)
    inverses = lax.all_gather(invert_blocks(owned, counted), "dp", axis=0, tiled=True)
    pre_inputs = apply_blocks(activations, inverses[:blocks_each])
    pre_grads = apply_blocks(gradients, inverses[blocks_each:])
    return (pre_inputs, pre_grads)


def solution(mesh):
    in_specs = (P("dp", None), P("dp", None), P("section", "dp", None), P("dp"))
    out_specs = (P("section", "dp", None), P("section", "dp", None))
    return jax.shard_map(
        on_device, mesh=mesh, in_specs=in_specs, out_specs=out_specs, check_vma=False
    )
```

time: 838 us -> 497 us (0.59)
  other arithmetic: 216 us -> 8.96 us
  waiting for transfers between devices: 408 us -> 351 us
  starting transfers between devices: 49.2 us -> 5.96 us
  matrix products: 103 us -> 59.8 us
  Pallas kernels: 0 us -> 21.1 us
  local copies, waits for them, and re-layouts: 23.7 us -> 14.4 us
    another operation x18 -> x0, other arithmetic: 188 us -> none  [the longest x10 104 us: invert_blocks(): lower = jnp.linalg.cholesky(damped)]
    ppermute x16 -> x6, waiting for transfers between devices: 91.9 us -> 32.7 us  [the longest x3 30.8 us: on_device(): arrived = lax.ppermute(result, 'section', [(stage, stage - 1)])]
    ppermute x16 -> x6, starting transfers between devices: 49.1 us -> 5.84 us  [the longest x3 2.94 us: on_device(): arrived = lax.ppermute(result, 'section', [(stage, stage + 1)])]
    dot_general x10 -> x6, matrix products: 82.7 us -> 48.8 us  [the longest x3 27.6 us: on_device(): lax.dot_general(gradients, full_weight, (((1,), (1,)), ((), ())), preferr...]
    pallas_call x0 -> x1, Pallas kernels: none -> 21.1 us  [invert_blocks(): pl.pallas_call(functools.partial(invert_kernel, count), out_shape=jax.Sha...]
    dynamic_update_slice x10 -> x0, other arithmetic: 13.3 us -> none  [the longest x5 8.57 us: retreat(): return (result, lax.dynamic_update_index_in_dim(kept, state, picked, 0))]
    another operation x19 -> x0, local copies, waits for them, and re-layouts: 8.82 us -> none
  transfers between devices with their start and end apart: 19 -> 9, of which waited for: 19 -> 5; matrix products, arithmetic and copies ran while one was open for 1% -> 1% of each run, Pallas kernels for 0% -> 0%
where the time goes in v1:
time: 497 us; the launch traced here: 496 us
  waiting for transfers between devices  351 us (71%)
  matrix products  59.8 us (12%)
  Pallas kernels  21.1 us (4%)
  blocking collectives  20.8 us (4%)
  local copies, waits for them, and re-layouts  14.4 us (3%)
  between operations  14 us (3%)
  other arithmetic  8.96 us (2%)
  starting transfers between devices  5.96 us (1%)
    all_gather x1, waiting for transfers between devices, on_device(): full_weight = lax.all_gather(weights, 'dp', axis=1, tiled=True)[0]  187 us
    reduce_scatter x1, waiting for transfers between devices, on_device(): owned = lax.psum_scatter(stacked, 'dp', scatter_dimension=0, tiled=True)  79 us
    all_gather x1, waiting for transfers between devices, on_device(): lax.all_gather(invert_blocks(owned, counted), 'dp', axis=0, tiled=True)  51.2 us
    ppermute x3, waiting for transfers between devices, on_device(): arrived = lax.ppermute(result, 'section', [(stage, stage - 1)])  30.8 us
    dot_general x3, matrix products, on_device(): lax.dot_general(gradients, full_weight, (((1,), (1,)), ((), ())), preferr...  27.6 us
    dot_general x3, matrix products, on_device(): jnp.dot(activation, full_weight, preferred_element_type=jnp.float32)  21.2 us
    pallas_call x1, Pallas kernels, invert_blocks(): pl.pallas_call(functools.partial(invert_kernel, count), out_shape=jax.Sha...  21.1 us
    psum x1, blocking collectives, on_device(): counted = lax.psum(jnp.sum(live.astype(jnp.float32)), 'dp')  20.8 us
  transfers between devices with their start and end apart: 9, of which 5 were waited for; matrix products, arithmetic and copies ran while one was open for 1% of the time, Pallas kernels for 0%

profile of v1, /device:TPU:0, one launch (start us, length us, event | category | flops | bytes accessed | tf_op | source)
XLA Modules:
  0.0 496.0 jit_solution(3450558446076509382)
XLA Ops:
  8.6 187.2 %all-gather.3.cloned.1.call-done = bf16[1,2560,2560]{2,1,0:T(8,128)(2,1)} async-done(((bf16[1,320,2560]{2,1,0:T(8,128)(2,1)}), bf16[1,2560,2560]{2,1,0:T(8,128)(2,1)}) %all-gather.3.cloned.1.call-update) | async-done | bytes 13107216 | tf_op jit(solution)/shard_map/all_gather | solution.py:111
  195.8 7.0 %fusion.27 = bf16[160,2560]{1,0:T(8,128)(2,1)S(1)} fusion(bf16[1,2560,2560]{2,1,0:T(8,128)(2,1)} %all-gather.3.cloned.1.call-done, bf16[160,2560]{1,0:T(8,128)(2,1)S(1)} %copy-done.2, f32[160]{0:T(256)S(1)} %add_rsqrt_fusion.3), kind=kOutput, calls=%fused_computation.18 | convolution fusion | flops 2099609600 | bytes 14746240 | tf_op jit(solution)/shard_map/dot_general | solution.py:118
  204.2 1.9 collective-permute-done
  206.5 7.1 %fusion.24 = bf16[160,2560]{1,0:T(8,128)(2,1)S(1)} fusion(bf16[1,2560,2560]{2,1,0:T(8,128)(2,1)} %all-gather.3.cloned.1.call-done, bf16[160,2560]{1,0:T(8,128)(2,1)S(1)} %get-tuple-element.17, f32[160]{0:T(256)S(1)} %add_rsqrt_fusion.2), kind=kOutput, calls=%fused_computation.17 | convolution fusion | flops 2099609600 | bytes 14746240 | tf_op jit(solution)/shard_map/dot_general | solution.py:118
  214.7 7.1 %fusion.21 = bf16[160,2560]{1,0:T(8,128)(2,1)S(1)} fusion(bf16[1,2560,2560]{2,1,0:T(8,128)(2,1)} %all-gather.3.cloned.1.call-done, bf16[160,2560]{1,0:T(8,128)(2,1)S(1)} %get-tuple-element.15, f32[160]{0:T(256)S(1)} %add_rsqrt_fusion.1), kind=kOutput, calls=%fused_computation.16 | convolution fusion | flops 2099609600 | bytes 14746240 | tf_op jit(solution)/shard_map/dot_general | solution.py:118
  223.0 9.2 %fusion.37 = (f32[160]{0:T(256)S(1)}, f32[160,2560]{1,0:T(8,128)S(1)}) fusion(bf16[160,2560]{1,0:T(8,128)(2,1)S(1)} %get-tuple-element.13, f32[160]{0:T(256)S(1)} %add_rsqrt_fusion, bf16[160,2560]{1,0:T(8,128)(2,1)S(1)} %copy-done.1, bf16[1,2560,2560]{2,1,0:T(8,128)(2,1)} %all-gather.3.cloned.1.call-done), kind=kOutput, calls=%fused_computation.34 | convolution fusion | flops 2098790272 | bytes 16385280 | tf_op jit(solution)/shard_map/dot_general | solution.py:127
  233.7 9.2 %fusion.42 = (f32[160]{0:T(256)S(1)}, f32[160,2560]{1,0:T(8,128)S(1)}) fusion(bf16[160,2560]{1,0:T(8,128)(2,1)S(1)} %get-tuple-element.13, f32[160]{0:T(256)S(1)} %add_rsqrt_fusion, bf16[160,2560]{1,0:T(8,128)(2,1)S(1)} %broadcast_select_fusion.5, bf16[1,2560,2560]{2,1,0:T(8,128)(2,1)} %all-gather.3.cloned.1.call-done), kind=kOutput, calls=%fused_computation.39 | convolution fusion | flops 2098790272 | bytes 16385280 | tf_op jit(solution)/shard_map/dot_general | solution.py:127
  244.2 9.2 %fusion.47 = (f32[160]{0:T(256)S(1)}, f32[160,2560]{1,0:T(8,128)S(1)}) fusion(bf16[160,2560]{1,0:T(8,128)(2,1)S(1)} %get-tuple-element.13, f32[160]{0:T(256)S(1)} %add_rsqrt_fusion, bf16[160,2560]{1,0:T(8,128)(2,1)S(1)} %broadcast_select_fusion.3, bf16[1,2560,2560]{2,1,0:T(8,128)(2,1)} %all-gather.3.cloned.1.call-done), kind=kOutput, calls=%fused_computation.44 | convolution fusion | flops 2098790272 | bytes 16385280 | tf_op jit(solution)/shard_map/dot_general | solution.py:127
  255.4 30.8 %collective-permute-done.5 = bf16[160,2560]{1,0:T(8,128)(2,1)} collective-permute-done((bf16[160,2560]{1,0:T(8,128)(2,1)S(1)}, bf16[160,2560]{1,0:T(8,128)(2,1)}, u32[]{:S(2)}, u32[]{:S(2)}) %collective-permute-start.5) | collective-permute-done | bytes 819232 | tf_op jit(solution)/shard_map/ppermute | solution.py:132
  286.2 2.6 broadcast_select_fusion.1
  288.8 2.5 reshape.115
  291.3 2.8 fusion.61
  294.1 3.5 reshape.114
  297.6 2.8 fusion.63
  300.4 2.7 pad_maximum_fusion
  303.8 20.8 %psum.7.counted_ref = f32[1,1]{1,0:T(1,128)} all-reduce(f32[1,1]{1,0:T(1,128)} %bitcast), channel_id=1, replica_groups=mesh['section'=4,'dp'=8] {'dp'}, use_global_device_ids=true, to_apply=%region_1.0 | all-reduce | flops 1 | bytes 8 | tf_op jit(solution)/shard_map/psum | solution.py:110
  324.7 79.0 %reduce-scatter.2.cloned.1.call-done.blocks_ref = f32[4,160,160]{2,1,0:T(8,128)} async-done(((f32[32,160,160]{2,1,0:T(8,128)}), f32[4,160,160]{2,1,0:T(8,128)}) %reduce-scatter.2.cloned.1.call-update) | async-done | bytes 409616 | tf_op jit(solution)/shard_map/reduce_scatter | solution.py:146
  404.8 21.1 %shard_map.59 = bf16[4,160,160]{2,1,0:T(8,128)(2,1)} custom-call(f32[1,1]{1,0:T(1,128)} %psum.7.counted_ref, f32[4,160,160]{2,1,0:T(8,128)S(1)} %copy-done), custom_call_target="tpu_custom_call" | custom-call | tf_op jit(solution)/shard_map/pallas_call | solution.py:81
  425.9 1.7 reshape.117
  427.6 1.7 reshape.116
  429.2 51.2 %all-gather.5.cloned.1.call-done = bf16[32,160,160]{2,1,0:T(8,128)(2,1)} async-done(((bf16[4,160,160]{2,1,0:T(8,128)(2,1)}), bf16[32,160,160]{2,1,0:T(8,128)(2,1)}) %all-gather.5.cloned.1.call-update) | async-done | bytes 1638416 | tf_op jit(solution)/shard_map/all_gather | solution.py:147
  480.5 3.2 convolution_convert_fusion
  483.7 2.3 copy.35
  486.0 2.1 convolution_convert_fusion.1
  (46 shorter events, 13.3 us)
Async XLA Ops:
  7.2 1.1 copy-start.2
  7.2 188.6 %all-gather.3.cloned.1.call-start = ((), (), s32[]{:S(2)}) async-start(), calls=%async_computation.1 | async-start | bytes 14745600 | tf_op jit(solution)/shard_map/all_gather | solution.py:111
  7.9 395.8 %reduce-scatter.2.cloned.1.call-start = ((), (), s32[]{:S(2)}) async-start(), calls=%async_computation.2 | async-start | bytes 5898240 | tf_op jit(solution)/shard_map/reduce_scatter | solution.py:146
  202.8 3.3 collective-permute-start
  213.5 0.7 collective-permute-start.1
  221.7 1.3 copy-start.1
  221.7 0.9 collective-permute-start.2
  232.7 0.9 collective-permute-start.3
  243.4 0.7 collective-permute-start.4
  253.4 1.8 copy-start.4
  253.9 32.3 %collective-permute-start.5 = (bf16[160,2560]{1,0:T(8,128)(2,1)S(1)}, bf16[160,2560]{1,0:T(8,128)(2,1)}, u32[]{:S(2)}, u32[]{:S(2)}) collective-permute-start(bf16[160,2560]{1,0:T(8,128)(2,1)S(1)} %fusion.51), channel_id=1, source_target_pairs={{8,0},{9,1},{10,2},{11,3},{12,4},{13,5},{14,6},{15,7}} | collective-permute-start | bytes 2457608 | tf_op jit(solution)/shard_map/ppermute | solution.py:132
  303.1 122.8 %copy-start.3 = (bf16[160,2560]{1,0:T(8,128)(2,1)S(1)}, bf16[160,2560]{1,0:T(8,128)(2,1)}, u32[]{:S(2)}) copy-start(bf16[160,2560]{1,0:T(8,128)(2,1)} %get-tuple-element.19) | copy-start | bytes 2457604
  303.1 177.4 %all-gather.5.cloned.1.call-start = ((), (), s32[]{:S(2)}) async-start(), calls=%async_computation.3 | async-start | bytes 2949120 | tf_op jit(solution)/shard_map/all_gather | solution.py:147
  403.7 1.1 copy-start
Sparse Core Ops, SparseCore 0:
  10.2 185.5 all-gather.2
  303.2 100.3 reduce-scatter.1
  426.0 54.4 all-gather.4

commit v2 on v1

--- a/solution.py
+++ b/solution.py
@@ -64,34 +64,119 @@
                 work[m, at, at] = -inverse
 
 
-def invert_kernel(count, counted_ref, blocks_ref, out_ref, work, packed):
-    scale = 1.0 / counted_ref[0, 0]
+def invert_kernel(count, blocks_ref, out_ref, work, packed):
+    scale = 1.0 / blocks_ref[0, BLOCK : BLOCK + 1, :]
     diagonal = lax.broadcasted_iota(jnp.int32, (BLOCK, BLOCK), 0) == lax.broadcasted_iota(
         jnp.int32, (BLOCK, BLOCK), 1
     )
     for m in range(count):
-        work[m] = blocks_ref[m] * scale + jnp.where(diagonal, damping, 0.0)
+        work[m] = blocks_ref[m, :BLOCK, :] * scale + jnp.where(diagonal, damping, 0.0)
     invert_in_place(work, packed, count)
     for m in range(count):
         out_ref[m] = (-work[m]).astype(jnp.bfloat16)
 
 
-def invert_blocks(blocks, counted):
+def invert_blocks(blocks):
     count = blocks.shape[0]
+    shape = (count, BLOCK, BLOCK)
     return pl.pallas_call(
         functools.partial(invert_kernel, count),
-        out_shape=jax.ShapeDtypeStruct(blocks.shape, jnp.bfloat16),
-        in_specs=[
-            pl.BlockSpec(memory_space=pltpu.SMEM),
-            pl.BlockSpec(memory_space=pltpu.VMEM),
-        ],
+        out_shape=jax.ShapeDtypeStruct(shape, jnp.bfloat16),
+        in_specs=[pl.BlockSpec(memory_space=pltpu.VMEM)],
         out_specs=pl.BlockSpec(memory_space=pltpu.VMEM),
         scratch_shapes=[
-            pltpu.VMEM(blocks.shape, jnp.float32),
+            pltpu.VMEM(shape, jnp.float32),
             pltpu.VMEM((PANEL, LANES), jnp.float32),
         ],
         compiler_params=pltpu.CompilerParams(vmem_limit_bytes=32 * 1024 * 1024),
-    )(counted.reshape(1, 1), blocks)
+    )(blocks)
+
+
+def ring_device(place, count):
+    back = lax.div(place, count // 2)
+    return (1 - back) * (2 * place) + back * (2 * (count - 1 - place) + 1)
+
+
+def ring_place(index, count):
+    back = lax.rem(index, 2)
+    row = lax.div(index, 2)
+    return (1 - back) * row + back * (count - 1 - row)
+
+
+def ring_kernel(count, own_ref, out_ref, local_sem, send_sem, recv_sem):
+    rows = own_ref.shape[0]
+    first = rows // 32 * 16
+    starts, sizes = (0, first), (first, rows - first)
+    me = lax.axis_index("dp")
+    place = ring_place(me, count)
+    targets = [
+        ring_device(lax.rem(place + 1, count), count),
+        ring_device(lax.rem(place + count - 1, count), count),
+    ]
+    barrier = pltpu.get_barrier_semaphore()
+    for target in targets:
+        pl.semaphore_signal(
+            barrier, inc=1, device_id={"dp": target}, device_id_type=pl.DeviceIdType.MESH
+        )
+    pl.semaphore_wait(barrier, 2)
+
+    def part(owner, piece):
+        return out_ref.at[pl.ds(pl.multiple_of(owner * rows + starts[piece], 16), sizes[piece])]
+
+    own_copy = pltpu.make_async_copy(
+        own_ref, out_ref.at[pl.ds(pl.multiple_of(me * rows, 16), rows)], local_sem
+    )
+    steps = count // 2
+    copies = {}
+    waited = set()
+    for step in range(steps):
+        for piece in range(2):
+            for way in range(2):
+                if step == steps - 1 and piece != way:
+                    continue
+                travelled = lax.rem(place + (count - step if way == 0 else step), count)
+                owner = ring_device(travelled, count)
+                if step == 0:
+                    source = own_ref.at[pl.ds(starts[piece], sizes[piece])]
+                else:
+                    copies[step - 1, piece, way].wait_recv()
+                    waited.add((step - 1, piece, way))
+                    source = part(owner, piece)
+                copy = pltpu.make_async_remote_copy(
+                    src_ref=source,
+                    dst_ref=part(owner, piece),
+                    send_sem=send_sem.at[step, piece, way],
+                    recv_sem=recv_sem.at[step, piece, way],
+                    device_id={"dp": targets[way]},
+                    device_id_type=pl.DeviceIdType.MESH,
+                )
+                copy.start()
+                copies[step, piece, way] = copy
+        if step == 0:
+            own_copy.start()
+    for key, copy in copies.items():
+        if key not in waited:
+            copy.wait_recv()
+    for copy in copies.values():
+        copy.wait_send()
+    own_copy.wait()
+
+
+def ring_gather(own, collective_id):
+    count = lax.axis_size("dp")
+    rows, columns = own.shape
+    return pl.pallas_call(
+        functools.partial(ring_kernel, count),
+        out_shape=jax.ShapeDtypeStruct((count * rows, columns), own.dtype),
+        in_specs=[pl.BlockSpec(memory_space=pl.ANY)],
+        out_specs=pl.BlockSpec(memory_space=pl.ANY),
+        scratch_shapes=[
+            pltpu.SemaphoreType.DMA,
+            pltpu.SemaphoreType.DMA((count // 2, 2, 2)),
+            pltpu.SemaphoreType.DMA((count // 2, 2, 2)),
+        ],
+        compiler_params=pltpu.CompilerParams(collective_id=collective_id, has_side_effects=True),
+    )(own)
 
 
 def apply_blocks(values, inverse):
@@ -107,8 +192,8 @@
     micro_count = lengths.shape[0]
     batch_rows = token_count // micro_count
     live = (jnp.arange(batch_rows)[None, :] < lengths[:, None]).reshape(token_count, 1)
-    counted = lax.psum(jnp.sum(live.astype(jnp.float32)), "dp")
-    full_weight = lax.all_gather(weights, "dp", axis=1, tiled=True)[0]
+    counted = jnp.sum(live.astype(jnp.float32))
+    full_weight = ring_gather(weights[0], 0)
 
     hidden = inputs
     for stage in range(section_count - 1):
@@ -143,8 +228,11 @@
         "tbi,tbj->bij", masked_grad, masked_grad, preferred_element_type=jnp.float32
     )
     stacked = jnp.concatenate([gram_act, gram_grad], axis=0)
+    counts = jnp.full((stacked.shape[0], 8, BLOCK), counted, jnp.float32)
+    stacked = jnp.concatenate([stacked, counts], axis=1)
     owned = lax.psum_scatter(stacked, "dp", scatter_dimension=0, tiled=True)
-    inverses = lax.all_gather(invert_blocks(owned, counted), "dp", axis=0, tiled=True)
+    inverse = invert_blocks(owned)
+    inverses = ring_gather(inverse.reshape(-1, BLOCK), 1).reshape(-1, BLOCK, BLOCK)
     pre_inputs = apply_blocks(activations, inverses[:blocks_each])
     pre_grads = apply_blocks(gradients, inverses[blocks_each:])
     return (pre_inputs, pre_grads)

time: 497 us -> 419 us (0.84)
  waiting for transfers between devices: 351 us -> 132 us
  Pallas kernels: 21.1 us -> 179 us
  blocking collectives: 20.8 us -> 0 us
  local copies, waits for them, and re-layouts: 14.4 us -> 20 us
    all_gather x2 -> x0, waiting for transfers between devices: 238 us -> none  [the longest x1 187 us: on_device(): full_weight = lax.all_gather(weights, 'dp', axis=1, tiled=True)[0]]
    pallas_call x0 -> x2, Pallas kernels: none -> 159 us  [ring_gather(): pl.pallas_call(functools.partial(ring_kernel, count), out_shape=jax.Shape...]
    psum x1 -> x0, blocking collectives: 20.8 us -> none  [on_device(): counted = lax.psum(jnp.sum(live.astype(jnp.float32)), 'dp')]
    reduce_scatter x1, waiting for transfers between devices: 79 us -> 99.4 us  [on_device(): owned = lax.psum_scatter(stacked, 'dp', scatter_dimension=0, tiled=True)]
  transfers between devices with their start and end apart: 9 -> 7, of which waited for: 5 -> 3; matrix products, arithmetic and copies ran while one was open for 1% -> 1% of each run, Pallas kernels for 0% -> 0%
where the time goes in v2:
time: 419 us
  Pallas kernels  179 us (43%)
  waiting for transfers between devices  132 us (32%)
  matrix products  58.3 us (14%)
  local copies, waits for them, and re-layouts  20 us (5%)
  between operations  14.3 us (3%)
  other arithmetic  9.68 us (2%)
  starting transfers between devices  5.84 us (1%)
    pallas_call x2, Pallas kernels, ring_gather(): pl.pallas_call(functools.partial(ring_kernel, count), out_shape=jax.Shape...  159 us
    reduce_scatter x1, waiting for transfers between devices, on_device(): owned = lax.psum_scatter(stacked, 'dp', scatter_dimension=0, tiled=True)  99.4 us
    ppermute x3, waiting for transfers between devices, on_device(): arrived = lax.ppermute(result, 'section', [(stage, stage - 1)])  30.2 us
    dot_general x3, matrix products, on_device(): lax.dot_general(gradients, full_weight, (((1,), (1,)), ((), ())), preferr...  27.6 us
    dot_general x3, matrix products, on_device(): jnp.dot(activation, full_weight, preferred_element_type=jnp.float32)  21.2 us
    pallas_call x1, Pallas kernels, invert_blocks(): pl.pallas_call(functools.partial(invert_kernel, count), out_shape=jax.Sha...  19.7 us
  transfers between devices with their start and end apart: 7, of which 3 were waited for; matrix products, arithmetic and copies ran while one was open for 1% of the time, Pallas kernels for 0%

profile of v2, /device:TPU:0, one launch (start us, length us, event | category | flops | bytes accessed | tf_op | source)
XLA Modules:
  0.0 418.8 jit_solution(16031691015821084105)
XLA Ops:
  7.2 130.3 %shard_map.59 = bf16[2560,2560]{1,0:T(8,128)(2,1)} custom-call(bf16[320,2560]{1,0:T(8,128)(2,1)} %bitcast.26), custom_call_target="tpu_custom_call" | custom-call | tf_op jit(solution)/shard_map/pallas_call | solution.py:168
  137.8 7.1 %fusion = bf16[160,2560]{1,0:T(8,128)(2,1)S(1)} fusion(bf16[2560,2560]{1,0:T(8,128)(2,1)} %shard_map.59, bf16[160,2560]{1,0:T(8,128)(2,1)S(1)} %copy-done.4, f32[160]{0:T(256)S(1)} %add_rsqrt_fusion.3), kind=kOutput, calls=%fused_computation.5 | convolution fusion | flops 2099609600 | bytes 14746240 | tf_op jit(solution)/shard_map/dot_general | solution.py:203
  146.2 1.9 collective-permute-done
  148.5 7.1 %fusion.1 = bf16[160,2560]{1,0:T(8,128)(2,1)S(1)} fusion(bf16[2560,2560]{1,0:T(8,128)(2,1)} %shard_map.59, bf16[160,2560]{1,0:T(8,128)(2,1)S(1)} %get-tuple-element.15, f32[160]{0:T(256)S(1)} %add_rsqrt_fusion.2), kind=kOutput, calls=%fused_computation.6 | convolution fusion | flops 2099609600 | bytes 14746240 | tf_op jit(solution)/shard_map/dot_general | solution.py:203
  156.7 7.1 %fusion.2 = bf16[160,2560]{1,0:T(8,128)(2,1)S(1)} fusion(bf16[2560,2560]{1,0:T(8,128)(2,1)} %shard_map.59, bf16[160,2560]{1,0:T(8,128)(2,1)S(1)} %get-tuple-element.13, f32[160]{0:T(256)S(1)} %add_rsqrt_fusion.1), kind=kOutput, calls=%fused_computation.7 | convolution fusion | flops 2099609600 | bytes 14746240 | tf_op jit(solution)/shard_map/dot_general | solution.py:203
  165.0 9.2 %fusion.10 = (f32[160]{0:T(256)S(1)}, f32[160,2560]{1,0:T(8,128)S(1)}) fusion(bf16[160,2560]{1,0:T(8,128)(2,1)S(1)} %get-tuple-element.11, f32[160]{0:T(256)S(1)} %add_rsqrt_fusion, bf16[160,2560]{1,0:T(8,128)(2,1)S(1)} %copy-done.2, bf16[2560,2560]{1,0:T(8,128)(2,1)} %shard_map.59), kind=kOutput, calls=%fused_computation.23 | convolution fusion | flops 2098790272 | bytes 16385280 | tf_op jit(solution)/shard_map/dot_general | solution.py:212
  175.7 9.2 %fusion.15 = (f32[160]{0:T(256)S(1)}, f32[160,2560]{1,0:T(8,128)S(1)}) fusion(bf16[160,2560]{1,0:T(8,128)(2,1)S(1)} %get-tuple-element.11, f32[160]{0:T(256)S(1)} %add_rsqrt_fusion, bf16[160,2560]{1,0:T(8,128)(2,1)S(1)} %broadcast_select_fusion.5, bf16[2560,2560]{1,0:T(8,128)(2,1)} %shard_map.59), kind=kOutput, calls=%fused_computation.28 | convolution fusion | flops 2098790272 | bytes 16385280 | tf_op jit(solution)/shard_map/dot_general | solution.py:212
  186.2 9.2 %fusion.20 = (f32[160]{0:T(256)S(1)}, f32[160,2560]{1,0:T(8,128)S(1)}) fusion(bf16[160,2560]{1,0:T(8,128)(2,1)S(1)} %get-tuple-element.11, f32[160]{0:T(256)S(1)} %add_rsqrt_fusion, bf16[160,2560]{1,0:T(8,128)(2,1)S(1)} %broadcast_select_fusion.3, bf16[2560,2560]{1,0:T(8,128)(2,1)} %shard_map.59), kind=kOutput, calls=%fused_computation.33 | convolution fusion | flops 2098790272 | bytes 16385280 | tf_op jit(solution)/shard_map/dot_general | solution.py:212
  198.1 30.2 %collective-permute-done.5 = bf16[160,2560]{1,0:T(8,128)(2,1)} collective-permute-done((bf16[160,2560]{1,0:T(8,128)(2,1)S(1)}, bf16[160,2560]{1,0:T(8,128)(2,1)}, u32[]{:S(2)}, u32[]{:S(2)}) %collective-permute-start.5) | collective-permute-done | bytes 819232 | tf_op jit(solution)/shard_map/ppermute | solution.py:217
  228.2 2.6 broadcast_select_fusion.1
  230.8 2.5 reshape.117
  233.3 2.8 fusion.34
  236.2 3.5 reshape.116
  239.6 2.8 fusion.36
  242.5 3.4 select_maximum_fusion
  247.0 2.5 reshape.120
  251.4 99.4 %reduce-scatter.2.cloned.1.call-done.blocks_ref = f32[4,168,160]{2,1,0:T(8,128)} async-done(((f32[32,168,160]{2,1,0:T(8,128)}), f32[4,168,160]{2,1,0:T(8,128)}) %reduce-scatter.2.cloned.1.call-update) | async-done | bytes 430096 | tf_op jit(solution)/shard_map/reduce_scatter | solution.py:233
  351.9 19.7 %shard_map.60 = bf16[4,160,160]{2,1,0:T(8,128)(2,1)S(1)} custom-call(f32[4,168,160]{2,1,0:T(8,128)S(1)} %copy-done.1), custom_call_target="tpu_custom_call" | custom-call | tf_op jit(solution)/shard_map/pallas_call | solution.py:82
  372.3 29.1 %shard_map.61 = bf16[5120,160]{1,0:T(8,128)(2,1)} custom-call(bf16[640,160]{1,0:T(8,128)(2,1)} %bitcast.21), custom_call_target="tpu_custom_call" | custom-call | tf_op jit(solution)/shard_map/pallas_call | solution.py:168
  401.4 2.0 fusion.45
  403.5 1.9 convolution_convert_fusion
  405.5 2.3 copy.29
  407.7 1.9 convolution_convert_fusion.1
  409.6 2.3 copy.28
  (46 shorter events, 14.6 us)
Async XLA Ops:
  7.2 343.7 %reduce-scatter.2.cloned.1.call-start = ((), (), s32[]{:S(2)}) async-start(), calls=%async_computation.1 | async-start | bytes 6193152 | tf_op jit(solution)/shard_map/reduce_scatter | solution.py:233
  7.2 130.3 %copy-start.4 = (bf16[160,2560]{1,0:T(8,128)(2,1)S(1)}, bf16[160,2560]{1,0:T(8,128)(2,1)}, u32[]{:S(2)}) copy-start(bf16[160,2560]{1,0:T(8,128)(2,1)} %param.4) | copy-start | bytes 2457604
  144.9 3.2 collective-permute-start
  155.6 0.7 collective-permute-start.1
  163.7 1.3 copy-start.2
  163.8 0.9 collective-permute-start.2
  174.7 0.9 collective-permute-start.3
  185.4 0.7 collective-permute-start.4
  195.5 1.8 copy-start.6
  195.9 32.3 %collective-permute-start.5 = (bf16[160,2560]{1,0:T(8,128)(2,1)S(1)}, bf16[160,2560]{1,0:T(8,128)(2,1)}, u32[]{:S(2)}, u32[]{:S(2)}) collective-permute-start(bf16[160,2560]{1,0:T(8,128)(2,1)S(1)} %fusion.24), channel_id=1, source_target_pairs={{8,0},{9,1},{10,2},{11,3},{12,4},{13,5},{14,6},{15,7}} | collective-permute-start | bytes 2457608 | tf_op jit(solution)/shard_map/ppermute | solution.py:217
  245.9 1.1 copy-start.5
  350.8 1.1 copy-start.1
  371.6 0.7 copy-start
  401.4 2.1 copy-start.3
Sparse Core Ops, SparseCore 0:
  246.0 104.7 reduce-scatter.1

commit v3 on v2

--- a/solution.py
+++ b/solution.py
@@ -179,6 +179,106 @@
     )(own)
 
 
+def exchange_kernel(
+    count, sent_ref, live_ref, out_ref, held, held_live, work, packed, local_sem, send_sem, recv_sem
+):
+    tokens, columns = held.shape[1:]
+    me = lax.axis_index("dp")
+    barrier = pltpu.get_barrier_semaphore()
+    for offset in range(1, count):
+        pl.semaphore_signal(
+            barrier,
+            inc=1,
+            device_id={"dp": lax.rem(me + offset, count)},
+            device_id_type=pl.DeviceIdType.MESH,
+        )
+    pl.semaphore_wait(barrier, count - 1)
+
+    def group(owner):
+        kind = lax.div(owner, count // 2)
+        column = lax.rem(owner, count // 2) * columns
+        return sent_ref.at[kind, :, pl.ds(pl.multiple_of(column, LANES), columns)]
+
+    def remote(source, target, offset, which):
+        return pltpu.make_async_remote_copy(
+            src_ref=source,
+            dst_ref=target,
+            send_sem=send_sem.at[offset - 1, which],
+            recv_sem=recv_sem.at[offset - 1, which],
+            device_id={"dp": lax.rem(me + offset, count)},
+            device_id_type=pl.DeviceIdType.MESH,
+        )
+
+    copies = {}
+    for offset in range(1, count):
+        copies[offset, 0] = remote(
+            group(lax.rem(me + offset, count)), held.at[me], offset, 0
+        )
+        copies[offset, 1] = remote(live_ref, held_live.at[me], offset, 1)
+        copies[offset, 1].start()
+        copies[offset, 0].start()
+    own_copy = pltpu.make_async_copy(group(me), held.at[me], local_sem)
+    own_copy.start()
+    work[...] = jnp.zeros_like(work)
+    total = live_ref[...]
+
+    for offset in range(count):
+        sender = lax.rem(me + count - offset, count)
+        if offset == 0:
+            own_copy.wait()
+        else:
+            copies[offset, 0].wait_recv()
+            copies[offset, 1].wait_recv()
+            total = total + held_live[sender]
+        values = held[sender]
+        for m in range(PACK):
+            block = values[:, m * BLOCK : (m + 1) * BLOCK]
+            work[m] += lax.dot_general(
+                block, block, (((0,), (0,)), ((), ())), preferred_element_type=jnp.float32
+            )
+
+    scale = 1.0 / total[0:1, 0:1]
+    diagonal = lax.broadcasted_iota(jnp.int32, (BLOCK, BLOCK), 0) == lax.broadcasted_iota(
+        jnp.int32, (BLOCK, BLOCK), 1
+    )
+    for m in range(PACK):
+        work[m] = work[m] * scale + jnp.where(diagonal, damping, 0.0)
+    invert_in_place(work, packed, PACK)
+    for m in range(PACK):
+        out_ref[:, m * BLOCK : (m + 1) * BLOCK] = (-work[m]).astype(jnp.bfloat16)
+    for copy in copies.values():
+        copy.wait_send()
+
+
+def exchange_and_invert(sent, counted, collective_id):
+    count = lax.axis_size("dp")
+    tokens = sent.shape[1]
+    columns = PACK * BLOCK
+    return pl.pallas_call(
+        functools.partial(exchange_kernel, count),
+        out_shape=jax.ShapeDtypeStruct((BLOCK, columns), jnp.bfloat16),
+        in_specs=[
+            pl.BlockSpec(memory_space=pl.ANY),
+            pl.BlockSpec(memory_space=pltpu.VMEM),
+        ],
+        out_specs=pl.BlockSpec(memory_space=pltpu.VMEM),
+        scratch_shapes=[
+            pltpu.VMEM((count, tokens, columns), jnp.bfloat16),
+            pltpu.VMEM((count, 8, LANES), jnp.float32),
+            pltpu.VMEM((PACK, BLOCK, BLOCK), jnp.float32),
+            pltpu.VMEM((PANEL, LANES), jnp.float32),
+            pltpu.SemaphoreType.DMA,
+            pltpu.SemaphoreType.DMA((count - 1, 2)),
+            pltpu.SemaphoreType.DMA((count - 1, 2)),
+        ],
+        compiler_params=pltpu.CompilerParams(
+            collective_id=collective_id,
+            has_side_effects=True,
+            vmem_limit_bytes=32 * 1024 * 1024,
+        ),
+    )(sent, jnp.full((8, LANES), counted, jnp.float32))
+
+
 def apply_blocks(values, inverse):
     shaped = values.reshape(values.shape[0], inverse.shape[0], inverse.shape[1])
     result = jnp.einsum("tbi,bij->tbj", shaped, inverse, preferred_element_type=jnp.float32)
@@ -219,20 +319,27 @@
 
     blocks_each = width // BLOCK
     zero_value = jnp.zeros((), jnp.bfloat16)
-    masked_act = jnp.where(live, activations, zero_value).reshape(token_count, blocks_each, BLOCK)
-    masked_grad = jnp.where(live, gradients, zero_value).reshape(token_count, blocks_each, BLOCK)
-    gram_act = jnp.einsum(
-        "tbi,tbj->bij", masked_act, masked_act, preferred_element_type=jnp.float32
-    )
-    gram_grad = jnp.einsum(
-        "tbi,tbj->bij", masked_grad, masked_grad, preferred_element_type=jnp.float32
-    )
-    stacked = jnp.concatenate([gram_act, gram_grad], axis=0)
-    counts = jnp.full((stacked.shape[0], 8, BLOCK), counted, jnp.float32)
-    stacked = jnp.concatenate([stacked, counts], axis=1)
-    owned = lax.psum_scatter(stacked, "dp", scatter_dimension=0, tiled=True)
-    inverse = invert_blocks(owned)
-    inverses = ring_gather(inverse.reshape(-1, BLOCK), 1).reshape(-1, BLOCK, BLOCK)
+    dp_count = lax.axis_size("dp")
+    if 2 * blocks_each == PACK * dp_count and dp_count % 2 == 0:
+        sent = jnp.where(live[None], jnp.stack([activations, gradients]), zero_value)
+        inverse = exchange_and_invert(sent, counted, 2)
+        inverses = ring_gather(inverse, 1).reshape(dp_count, BLOCK, PACK, BLOCK)
+        inverses = jnp.swapaxes(inverses, 1, 2).reshape(-1, BLOCK, BLOCK)
+    else:
+        masked_act = jnp.where(live, activations, zero_value).reshape(token_count, blocks_each, BLOCK)
+        masked_grad = jnp.where(live, gradients, zero_value).reshape(token_count, blocks_each, BLOCK)
+        gram_act = jnp.einsum(
+            "tbi,tbj->bij", masked_act, masked_act, preferred_element_type=jnp.float32
+        )
+        gram_grad = jnp.einsum(
+            "tbi,tbj->bij", masked_grad, masked_grad, preferred_element_type=jnp.float32
+        )
+        stacked = jnp.concatenate([gram_act, gram_grad], axis=0)
+        counts = jnp.full((stacked.shape[0], 8, BLOCK), counted, jnp.float32)
+        stacked = jnp.concatenate([stacked, counts], axis=1)
+        owned = lax.psum_scatter(stacked, "dp", scatter_dimension=0, tiled=True)
+        inverse = invert_blocks(owned)
+        inverses = ring_gather(inverse.reshape(-1, BLOCK), 1).reshape(-1, BLOCK, BLOCK)
     pre_inputs = apply_blocks(activations, inverses[:blocks_each])
     pre_grads = apply_blocks(gradients, inverses[blocks_each:])
     return (pre_inputs, pre_grads)

time: 419 us -> 327 us (0.78)
  waiting for transfers between devices: 132 us -> 29.4 us
  Pallas kernels: 179 us -> 214 us
  between operations: 14.3 us -> 0.95 us
  matrix products: 58.3 us -> 52.5 us
  other arithmetic: 9.68 us -> 4.09 us
    reduce_scatter x1 -> x0, waiting for transfers between devices: 99.4 us -> none  [on_device(): owned = lax.psum_scatter(stacked, 'dp', scatter_dimension=0, tiled=True)]
    pallas_call x1, Pallas kernels: 19.7 us -> 49.6 us  [exchange_and_invert(): pl.pallas_call(functools.partial(exchange_kernel, count), out_shape=jax.S...]
    dot_general x2 -> x0, matrix products: 5.69 us -> none  [the longest x1 2.85 us: on_device(): jnp.einsum('tbi,tbj->bij', masked_grad, masked_grad, preferred_element_ty...]
    pallas_call x2, Pallas kernels: 159 us -> 164 us  [ring_gather(): pl.pallas_call(functools.partial(ring_kernel, count), out_shape=jax.Shape...]
  transfers between devices with their start and end apart: 7 -> 6, of which waited for: 3 -> 2; matrix products, arithmetic and copies ran while one was open for 1% -> 1% of each run, Pallas kernels for 0% -> 0%
where the time goes in v3:
time: 327 us; the launch traced here: 326 us
  Pallas kernels  214 us (65%)
  matrix products  52.5 us (16%)
  waiting for transfers between devices  29.4 us (9%)
  local copies, waits for them, and re-layouts  19.9 us (6%)
  starting transfers between devices  5.8 us (2%)
  other arithmetic  4.09 us (1%)
    pallas_call x2, Pallas kernels, ring_gather(): pl.pallas_call(functools.partial(ring_kernel, count), out_shape=jax.Shape...  164 us
    pallas_call x1, Pallas kernels, exchange_and_invert(): pl.pallas_call(functools.partial(exchange_kernel, count), out_shape=jax.S...  49.6 us
    dot_general x3, matrix products, on_device(): lax.dot_general(gradients, full_weight, (((1,), (1,)), ((), ())), preferr...  27.6 us
    ppermute x3, waiting for transfers between devices, on_device(): arrived = lax.ppermute(result, 'section', [(stage, stage - 1)])  27.5 us
    dot_general x3, matrix products, on_device(): jnp.dot(activation, full_weight, preferred_element_type=jnp.float32)  21.2 us
  transfers between devices with their start and end apart: 6, of which 2 were waited for; matrix products, arithmetic and copies ran while one was open for 1% of the time, Pallas kernels for 0%

profile of v3, /device:TPU:0, one launch (start us, length us, event | category | flops | bytes accessed | tf_op | source)
XLA Modules:
  0.0 326.4 jit_solution(11163649115321471302)
XLA Ops:
  0.6 130.3 %shard_map.59 = bf16[2560,2560]{1,0:T(8,128)(2,1)} custom-call(bf16[320,2560]{1,0:T(8,128)(2,1)} %bitcast.30), custom_call_target="tpu_custom_call" | custom-call | tf_op jit(solution)/shard_map/pallas_call | solution.py:168
  131.2 7.1 %fusion = bf16[160,2560]{1,0:T(8,128)(2,1)S(1)} fusion(bf16[2560,2560]{1,0:T(8,128)(2,1)} %shard_map.59, bf16[160,2560]{1,0:T(8,128)(2,1)S(1)} %copy-done.4, f32[160]{0:T(256)S(1)} %add_rsqrt_fusion.3), kind=kOutput, calls=%fused_computation.3 | convolution fusion | flops 2099609600 | bytes 14746240 | tf_op jit(solution)/shard_map/dot_general | solution.py:303
  138.3 1.3 collective-permute-start
  139.6 1.9 collective-permute-done
  141.9 7.1 %fusion.1 = bf16[160,2560]{1,0:T(8,128)(2,1)S(1)} fusion(bf16[2560,2560]{1,0:T(8,128)(2,1)} %shard_map.59, bf16[160,2560]{1,0:T(8,128)(2,1)S(1)} %get-tuple-element.11, f32[160]{0:T(256)S(1)} %add_rsqrt_fusion.2), kind=kOutput, calls=%fused_computation.4 | convolution fusion | flops 2099609600 | bytes 14746240 | tf_op jit(solution)/shard_map/dot_general | solution.py:303
  150.1 7.1 %fusion.2 = bf16[160,2560]{1,0:T(8,128)(2,1)S(1)} fusion(bf16[2560,2560]{1,0:T(8,128)(2,1)} %shard_map.59, bf16[160,2560]{1,0:T(8,128)(2,1)S(1)} %get-tuple-element.9, f32[160]{0:T(256)S(1)} %add_rsqrt_fusion.1), kind=kOutput, calls=%fused_computation.5 | convolution fusion | flops 2099609600 | bytes 14746240 | tf_op jit(solution)/shard_map/dot_general | solution.py:303
  158.4 9.2 %fusion.10 = (f32[160]{0:T(256)S(1)}, f32[160,2560]{1,0:T(8,128)S(1)}) fusion(bf16[160,2560]{1,0:T(8,128)(2,1)S(1)} %get-tuple-element.7, f32[160]{0:T(256)S(1)} %add_rsqrt_fusion, bf16[160,2560]{1,0:T(8,128)(2,1)S(1)} %copy-done.1, bf16[2560,2560]{1,0:T(8,128)(2,1)} %shard_map.59), kind=kOutput, calls=%fused_computation.21 | convolution fusion | flops 2098790272 | bytes 16385280 | tf_op jit(solution)/shard_map/dot_general | solution.py:312
  168.2 0.9 collective-permute-start.3
  169.2 9.2 %fusion.15 = (f32[160]{0:T(256)S(1)}, f32[160,2560]{1,0:T(8,128)S(1)}) fusion(bf16[160,2560]{1,0:T(8,128)(2,1)S(1)} %get-tuple-element.7, f32[160]{0:T(256)S(1)} %add_rsqrt_fusion, bf16[160,2560]{1,0:T(8,128)(2,1)S(1)} %broadcast_select_fusion.3, bf16[2560,2560]{1,0:T(8,128)(2,1)} %shard_map.59), kind=kOutput, calls=%fused_computation.26 | convolution fusion | flops 2098790272 | bytes 16385280 | tf_op jit(solution)/shard_map/dot_general | solution.py:312
  179.7 9.2 %fusion.20 = (f32[160]{0:T(256)S(1)}, f32[160,2560]{1,0:T(8,128)S(1)}) fusion(bf16[160,2560]{1,0:T(8,128)(2,1)S(1)} %get-tuple-element.7, f32[160]{0:T(256)S(1)} %add_rsqrt_fusion, bf16[160,2560]{1,0:T(8,128)(2,1)S(1)} %broadcast_select_fusion.1, bf16[2560,2560]{1,0:T(8,128)(2,1)} %shard_map.59), kind=kOutput, calls=%fused_computation.31 | convolution fusion | flops 2098790272 | bytes 16385280 | tf_op jit(solution)/shard_map/dot_general | solution.py:312
  189.4 1.3 collective-permute-start.5
  191.5 2.5 reshape.111
  194.0 27.5 %collective-permute-done.5 = bf16[160,2560]{1,0:T(8,128)(2,1)S(1)} collective-permute-done((bf16[160,2560]{1,0:T(8,128)(2,1)S(1)}, bf16[160,2560]{1,0:T(8,128)(2,1)S(1)}, u32[]{:S(2)}, u32[]{:S(2)}) %collective-permute-start.5) | collective-permute-done | bytes 819232 | tf_op jit(solution)/shard_map/ppermute | solution.py:317
  221.6 2.5 reshape.112
  225.0 49.6 %shard_map.60.own_ref = bf16[160,640]{1,0:T(8,128)(2,1)S(1)} custom-call(bf16[2,160,2560]{2,1,0:T(8,128)(2,1)S(1)} %maximum_select_fusion.sent_ref, f32[8,128]{1,0:T(8,128)S(1)} %broadcast_in_dim.12.live_ref), custom_call_target="tpu_custom_call" | custom-call | tf_op jit(solution)/shard_map/pallas_call | solution.py:257
  275.4 33.8 %shard_map.61 = bf16[1280,640]{1,0:T(8,128)(2,1)} custom-call(bf16[160,640]{1,0:T(8,128)(2,1)} %copy-done), custom_call_target="tpu_custom_call" | custom-call | tf_op jit(solution)/shard_map/pallas_call | solution.py:168
  309.2 3.5 %reshape.110 = bf16[8,160,4,160]{3,2,1,0:T(4,128)(2,1)S(1)} reshape(bf16[1280,640]{1,0:T(8,128)(2,1)} %shard_map.61) | data formatting | bytes 3276800 | tf_op jit(solution)/shard_map/reshape | solution.py:326
  312.7 2.4 fusion.40
  315.1 2.8 copy.14
  317.9 1.7 convolution_convert_fusion
  319.6 2.4 copy.17
  322.0 1.1 copy.12
  323.1 2.0 convolution_convert_fusion.1
  325.1 1.3 copy.16
  (41 shorter events, 7.8 us)
Async XLA Ops:
  0.6 130.3 %copy-start.4 = (bf16[160,2560]{1,0:T(8,128)(2,1)S(1)}, bf16[160,2560]{1,0:T(8,128)(2,1)}, u32[]{:S(2)}) copy-start(bf16[160,2560]{1,0:T(8,128)(2,1)} %param.4) | copy-start | bytes 2457604
  138.3 3.2 collective-permute-start
  149.0 0.7 collective-permute-start.1
  157.2 1.3 copy-start.1
  157.2 0.9 collective-permute-start.2
  168.2 0.9 collective-permute-start.3
  178.9 0.7 collective-permute-start.4
  188.9 1.8 copy-start.5
  189.4 32.2 %collective-permute-start.5 = (bf16[160,2560]{1,0:T(8,128)(2,1)S(1)}, bf16[160,2560]{1,0:T(8,128)(2,1)S(1)}, u32[]{:S(2)}, u32[]{:S(2)}) collective-permute-start(bf16[160,2560]{1,0:T(8,128)(2,1)S(1)} %fusion.24), channel_id=1, source_target_pairs={{8,0},{9,1},{10,2},{11,3},{12,4},{13,5},{14,6},{15,7}} | collective-permute-start | bytes 2457608 | tf_op jit(solution)/shard_map/ppermute | solution.py:317
  274.7 0.7 copy-start
  315.0 2.8 copy-start.3
  319.6 2.4 copy-start.2

commit v4 on v3

--- a/solution.py
+++ b/solution.py
@@ -279,6 +279,40 @@
     )(sent, jnp.full((8, LANES), counted, jnp.float32))
 
 
+def apply_kernel(act_ref, grad_ref, act_inverse_ref, grad_inverse_ref, first_ref, second_ref):
+    for values, inverse, result in (
+        (act_ref, act_inverse_ref, first_ref),
+        (grad_ref, grad_inverse_ref, second_ref),
+    ):
+        for m in range(PACK):
+            at = slice(m * BLOCK, (m + 1) * BLOCK)
+            result[0, :, at] = jnp.dot(
+                values[:, at], inverse[:, at], preferred_element_type=jnp.float32
+            ).astype(jnp.bfloat16)
+
+
+def apply_groups(activations, gradients, inverses):
+    tokens, width = activations.shape
+    columns = PACK * BLOCK
+    groups = width // columns
+    values = pl.BlockSpec((tokens, columns), lambda g: (0, g))
+    result = pl.BlockSpec((1, tokens, columns), lambda g: (0, 0, g))
+    shape = jax.ShapeDtypeStruct((1, tokens, width), jnp.bfloat16)
+    return pl.pallas_call(
+        apply_kernel,
+        grid=(groups,),
+        out_shape=(shape, shape),
+        in_specs=[
+            values,
+            values,
+            pl.BlockSpec((BLOCK, columns), lambda g: (g, 0)),
+            pl.BlockSpec((BLOCK, columns), lambda g: (g + groups, 0)),
+        ],
+        out_specs=(result, result),
+        compiler_params=pltpu.CompilerParams(vmem_limit_bytes=32 * 1024 * 1024),
+    )(activations, gradients, inverses, inverses)
+
+
 def apply_blocks(values, inverse):
     shaped = values.reshape(values.shape[0], inverse.shape[0], inverse.shape[1])
     result = jnp.einsum("tbi,bij->tbj", shaped, inverse, preferred_element_type=jnp.float32)
@@ -323,8 +357,7 @@
     if 2 * blocks_each == PACK * dp_count and dp_count % 2 == 0:
         sent = jnp.where(live[None], jnp.stack([activations, gradients]), zero_value)
         inverse = exchange_and_invert(sent, counted, 2)
-        inverses = ring_gather(inverse, 1).reshape(dp_count, BLOCK, PACK, BLOCK)
-        inverses = jnp.swapaxes(inverses, 1, 2).reshape(-1, BLOCK, BLOCK)
+        return apply_groups(activations, gradients, ring_gather(inverse, 1))
     else:
         masked_act = jnp.where(live, activations, zero_value).reshape(token_count, blocks_each, BLOCK)
         masked_grad = jnp.where(live, gradients, zero_value).reshape(token_count, blocks_each, BLOCK)

time: 327 us -> 313 us (0.957)
  local copies, waits for them, and re-layouts: 19.9 us -> 2.85 us
  Pallas kernels: 214 us -> 218 us
  matrix products: 52.5 us -> 48.8 us
    reshape x3 -> x0, local copies, waits for them, and re-layouts: 8.5 us -> none  [the longest x2 5 us: apply_blocks(): shaped = values.reshape(values.shape[0], inverse.shape[0], inverse.shape[1])]
    slice x3 -> x0, local copies, waits for them, and re-layouts: 6.27 us -> none  [the longest x2 5.17 us: on_device(): pre_grads = apply_blocks(gradients, inverses[blocks_each:])]
    dot_general x2 -> x0, matrix products: 3.69 us -> none  [apply_blocks(): jnp.einsum('tbi,bij->tbj', shaped, inverse, preferred_element_type=jnp.fl...]
  transfers between devices with their start and end apart: 6 -> 6, of which waited for: 2 -> 2; matrix products, arithmetic and copies ran while one was open for 1% -> 0% of each run, Pallas kernels for 0% -> 0%
where the time goes in v4:
time: 313 us; the launch traced here: 312 us
  Pallas kernels  218 us (70%)
  matrix products  48.8 us (16%)
  waiting for transfers between devices  31.9 us (10%)
  starting transfers between devices  5.8 us (2%)
  other arithmetic  4.12 us (1%)
    pallas_call x2, Pallas kernels, ring_gather(): pl.pallas_call(functools.partial(ring_kernel, count), out_shape=jax.Shape...  164 us
    pallas_call x1, Pallas kernels, exchange_and_invert(): pl.pallas_call(functools.partial(exchange_kernel, count), out_shape=jax.S...  50.2 us
    ppermute x3, waiting for transfers between devices, on_device(): arrived = lax.ppermute(result, 'section', [(stage, stage - 1)])  30 us
    dot_general x3, matrix products, on_device(): lax.dot_general(gradients, full_weight, (((1,), (1,)), ((), ())), preferr...  27.6 us
    dot_general x3, matrix products, on_device(): jnp.dot(activation, full_weight, preferred_element_type=jnp.float32)  21.2 us
  transfers between devices with their start and end apart: 6, of which 2 were waited for; matrix products, arithmetic and copies ran while one was open for 0% of the time, Pallas kernels for 0%

profile of v4, /device:TPU:0, one launch (start us, length us, event | category | flops | bytes accessed | tf_op | source)
XLA Modules:
  0.0 312.2 jit_solution(702122701200301881)
XLA Ops:
  0.6 130.3 %shard_map.59 = bf16[2560,2560]{1,0:T(8,128)(2,1)} custom-call(bf16[320,2560]{1,0:T(8,128)(2,1)} %bitcast.14), custom_call_target="tpu_custom_call" | custom-call | tf_op jit(solution)/shard_map/pallas_call | solution.py:168
  131.2 7.1 %fusion = bf16[160,2560]{1,0:T(8,128)(2,1)S(1)} fusion(bf16[2560,2560]{1,0:T(8,128)(2,1)} %shard_map.59, bf16[160,2560]{1,0:T(8,128)(2,1)S(1)} %copy-done.3, f32[160]{0:T(256)S(1)} %add_rsqrt_fusion.3), kind=kOutput, calls=%fused_computation.3 | convolution fusion | flops 2099609600 | bytes 14746240 | tf_op jit(solution)/shard_map/dot_general | solution.py:337
  138.3 1.3 collective-permute-start
  139.6 1.9 collective-permute-done
  141.9 7.1 %fusion.1 = bf16[160,2560]{1,0:T(8,128)(2,1)S(1)} fusion(bf16[2560,2560]{1,0:T(8,128)(2,1)} %shard_map.59, bf16[160,2560]{1,0:T(8,128)(2,1)S(1)} %get-tuple-element.7, f32[160]{0:T(256)S(1)} %add_rsqrt_fusion.2), kind=kOutput, calls=%fused_computation.4 | convolution fusion | flops 2099609600 | bytes 14746240 | tf_op jit(solution)/shard_map/dot_general | solution.py:337
  149.0 0.7 collective-permute-start.1
  150.1 7.1 %fusion.2 = bf16[160,2560]{1,0:T(8,128)(2,1)S(1)} fusion(bf16[2560,2560]{1,0:T(8,128)(2,1)} %shard_map.59, bf16[160,2560]{1,0:T(8,128)(2,1)S(1)} %get-tuple-element.5, f32[160]{0:T(256)S(1)} %add_rsqrt_fusion.1), kind=kOutput, calls=%fused_computation.5 | convolution fusion | flops 2099609600 | bytes 14746240 | tf_op jit(solution)/shard_map/dot_general | solution.py:337
  157.2 0.8 collective-permute-start.2
  158.4 9.2 %fusion.10 = (f32[160]{0:T(256)S(1)}, f32[160,2560]{1,0:T(8,128)S(1)}) fusion(bf16[160,2560]{1,0:T(8,128)(2,1)S(1)} %get-tuple-element.3, f32[160]{0:T(256)S(1)} %add_rsqrt_fusion, bf16[160,2560]{1,0:T(8,128)(2,1)S(1)} %copy-done.2, bf16[2560,2560]{1,0:T(8,128)(2,1)} %shard_map.59), kind=kOutput, calls=%fused_computation.21 | convolution fusion | flops 2098790272 | bytes 16385280 | tf_op jit(solution)/shard_map/dot_general | solution.py:346
  167.7 0.5 fusion.14
  168.1 0.9 collective-permute-start.3
  169.1 9.2 %fusion.15 = (f32[160]{0:T(256)S(1)}, f32[160,2560]{1,0:T(8,128)S(1)}) fusion(bf16[160,2560]{1,0:T(8,128)(2,1)S(1)} %get-tuple-element.3, f32[160]{0:T(256)S(1)} %add_rsqrt_fusion, bf16[160,2560]{1,0:T(8,128)(2,1)S(1)} %broadcast_select_fusion.3, bf16[2560,2560]{1,0:T(8,128)(2,1)} %shard_map.59), kind=kOutput, calls=%fused_computation.26 | convolution fusion | flops 2098790272 | bytes 16385280 | tf_op jit(solution)/shard_map/dot_general | solution.py:346
  178.8 0.7 collective-permute-start.4
  179.7 9.2 %fusion.20 = (f32[160]{0:T(256)S(1)}, f32[160,2560]{1,0:T(8,128)S(1)}) fusion(bf16[160,2560]{1,0:T(8,128)(2,1)S(1)} %get-tuple-element.3, f32[160]{0:T(256)S(1)} %add_rsqrt_fusion, bf16[160,2560]{1,0:T(8,128)(2,1)S(1)} %broadcast_select_fusion.1, bf16[2560,2560]{1,0:T(8,128)(2,1)} %shard_map.59), kind=kOutput, calls=%fused_computation.31 | convolution fusion | flops 2098790272 | bytes 16385280 | tf_op jit(solution)/shard_map/dot_general | solution.py:346
  188.9 0.5 fusion.24
  189.4 1.3 collective-permute-start.5
  190.9 0.7 convert_reduce_fusion
  191.6 30.0 %collective-permute-done.5 = bf16[160,2560]{1,0:T(8,128)(2,1)S(1)} collective-permute-done((bf16[160,2560]{1,0:T(8,128)(2,1)S(1)}, bf16[160,2560]{1,0:T(8,128)(2,1)S(1)}, u32[]{:S(2)}, u32[]{:S(2)}) %collective-permute-start.5) | collective-permute-done | bytes 819232 | tf_op jit(solution)/shard_map/ppermute | solution.py:351
  221.9 0.6 broadcast_in_dim.12.live_ref
  222.6 50.2 %shard_map.60.own_ref = bf16[160,640]{1,0:T(8,128)(2,1)S(1)} custom-call(bf16[2,160,2560]{2,1,0:T(8,128)(2,1)S(1)} %maximum_select_fusion.sent_ref, f32[8,128]{1,0:T(8,128)S(1)} %broadcast_in_dim.12.live_ref), custom_call_target="tpu_custom_call" | custom-call | tf_op jit(solution)/shard_map/pallas_call | solution.py:257
  272.8 0.7 copy-done.1
  273.4 34.1 %shard_map.61.act_inverse_ref.grad_inverse_ref = bf16[1280,640]{1,0:T(8,128)(2,1)} custom-call(bf16[160,640]{1,0:T(8,128)(2,1)} %copy-done.1), custom_call_target="tpu_custom_call" | custom-call | tf_op jit(solution)/shard_map/pallas_call | solution.py:168
  307.5 1.4 copy-done
  309.0 3.2 %shard_map.62 = (bf16[1,160,2560]{2,1,0:T(8,128)(2,1)}, bf16[1,160,2560]{2,1,0:T(8,128)(2,1)}) custom-call(bf16[160,2560]{1,0:T(8,128)(2,1)S(1)} %get-tuple-element.9.act_ref, bf16[160,2560]{1,0:T(8,128)(2,1)S(1)} %broadcast_select_fusion.grad_ref, bf16[1280,640]{1,0:T(8,128)(2,1)S(1)} %copy-done, bf16[1280,640]{1,0:T(8,128)(2,1)S(1)} %copy-done), custom_call_target="tpu_custom_call" | custom-call | tf_op jit(solution)/shard_map/pallas_call | solution.py:301
  (30 shorter events, 2.6 us)
Async XLA Ops:
  0.6 130.3 %copy-start.3 = (bf16[160,2560]{1,0:T(8,128)(2,1)S(1)}, bf16[160,2560]{1,0:T(8,128)(2,1)}, u32[]{:S(2)}) copy-start(bf16[160,2560]{1,0:T(8,128)(2,1)} %param.4) | copy-start | bytes 2457604
  138.3 3.2 %collective-permute-start = (bf16[160,2560]{1,0:T(8,128)(2,1)S(1)}, bf16[160,2560]{1,0:T(8,128)(2,1)S(1)}, u32[]{:S(2)}, u32[]{:S(2)}) collective-permute-start(bf16[160,2560]{1,0:T(8,128)(2,1)S(1)} %fusion), channel_id=1, source_target_pairs={{0,8},{1,9},{2,10},{3,11},{4,12},{5,13},{6,14},{7,15}} | collective-permute-start | bytes 2457608 | tf_op jit(solution)/shard_map/ppermute | solution.py:339
  149.0 0.7 collective-permute-start.1
  157.2 1.3 copy-start.2
  157.2 0.9 collective-permute-start.2
  168.1 0.9 collective-permute-start.3
  178.8 0.7 collective-permute-start.4
  188.9 1.8 copy-start.4
  189.4 32.2 %collective-permute-start.5 = (bf16[160,2560]{1,0:T(8,128)(2,1)S(1)}, bf16[160,2560]{1,0:T(8,128)(2,1)S(1)}, u32[]{:S(2)}, u32[]{:S(2)}) collective-permute-start(bf16[160,2560]{1,0:T(8,128)(2,1)S(1)} %get-tuple-element.8), channel_id=1, source_target_pairs={{8,0},{9,1},{10,2},{11,3},{12,4},{13,5},{14,6},{15,7}} | collective-permute-start | bytes 2457608 | tf_op jit(solution)/shard_map/ppermute | solution.py:351
  272.8 0.7 copy-start.1
  307.5 1.4 copy-start

commit v5 on v4

--- a/solution.py
+++ b/solution.py
@@ -162,14 +162,14 @@
     own_copy.wait()
 
 
-def ring_gather(own, collective_id):
+def ring_gather(own, collective_id, space=pl.ANY):
     count = lax.axis_size("dp")
     rows, columns = own.shape
     return pl.pallas_call(
         functools.partial(ring_kernel, count),
         out_shape=jax.ShapeDtypeStruct((count * rows, columns), own.dtype),
-        in_specs=[pl.BlockSpec(memory_space=pl.ANY)],
-        out_specs=pl.BlockSpec(memory_space=pl.ANY),
+        in_specs=[pl.BlockSpec(memory_space=space)],
+        out_specs=pl.BlockSpec(memory_space=space),
         scratch_shapes=[
             pltpu.SemaphoreType.DMA,
             pltpu.SemaphoreType.DMA((count // 2, 2, 2)),
@@ -357,7 +357,7 @@
     if 2 * blocks_each == PACK * dp_count and dp_count % 2 == 0:
         sent = jnp.where(live[None], jnp.stack([activations, gradients]), zero_value)
         inverse = exchange_and_invert(sent, counted, 2)
-        return apply_groups(activations, gradients, ring_gather(inverse, 1))
+        return apply_groups(activations, gradients, ring_gather(inverse, 1, pltpu.VMEM))
     else:
         masked_act = jnp.where(live, activations, zero_value).reshape(token_count, blocks_each, BLOCK)
         masked_grad = jnp.where(live, gradients, zero_value).reshape(token_count, blocks_each, BLOCK)

time: 313 us -> 314 us (level)
  no operation moved by 1% of the time
where the time goes in v5:
time: 314 us; the launch traced here: 313 us
  Pallas kernels  219 us (70%)
  matrix products  48.8 us (16%)
  waiting for transfers between devices  31.9 us (10%)
  starting transfers between devices  5.8 us (2%)
  other arithmetic  4.12 us (1%)
    pallas_call x2, Pallas kernels, ring_gather(): pl.pallas_call(functools.partial(ring_kernel, count), out_shape=jax.Shape...  166 us
    pallas_call x1, Pallas kernels, exchange_and_invert(): pl.pallas_call(functools.partial(exchange_kernel, count), out_shape=jax.S...  50.2 us
    ppermute x3, waiting for transfers between devices, on_device(): arrived = lax.ppermute(result, 'section', [(stage, stage - 1)])  30 us
    dot_general x3, matrix products, on_device(): lax.dot_general(gradients, full_weight, (((1,), (1,)), ((), ())), preferr...  27.6 us
    dot_general x3, matrix products, on_device(): jnp.dot(activation, full_weight, preferred_element_type=jnp.float32)  21.2 us
  transfers between devices with their start and end apart: 6, of which 2 were waited for; matrix products, arithmetic and copies ran while one was open for 0% of the time, Pallas kernels for 0%

profile of v5, /device:TPU:0, one launch (start us, length us, event | category | flops | bytes accessed | tf_op | source)
XLA Modules:
  0.0 313.3 jit_solution(10632635480616498570)
XLA Ops:
  0.6 130.3 %shard_map.59 = bf16[2560,2560]{1,0:T(8,128)(2,1)} custom-call(bf16[320,2560]{1,0:T(8,128)(2,1)} %bitcast.14), custom_call_target="tpu_custom_call" | custom-call | tf_op jit(solution)/shard_map/pallas_call | solution.py:168
  131.2 7.1 %fusion = bf16[160,2560]{1,0:T(8,128)(2,1)S(1)} fusion(bf16[2560,2560]{1,0:T(8,128)(2,1)} %shard_map.59, bf16[160,2560]{1,0:T(8,128)(2,1)S(1)} %copy-done.3, f32[160]{0:T(256)S(1)} %add_rsqrt_fusion.3), kind=kOutput, calls=%fused_computation.3 | convolution fusion | flops 2099609600 | bytes 14746240 | tf_op jit(solution)/shard_map/dot_general | solution.py:337
  138.3 1.3 collective-permute-start
  139.6 1.9 collective-permute-done
  141.9 7.1 %fusion.1 = bf16[160,2560]{1,0:T(8,128)(2,1)S(1)} fusion(bf16[2560,2560]{1,0:T(8,128)(2,1)} %shard_map.59, bf16[160,2560]{1,0:T(8,128)(2,1)S(1)} %get-tuple-element.7, f32[160]{0:T(256)S(1)} %add_rsqrt_fusion.2), kind=kOutput, calls=%fused_computation.4 | convolution fusion | flops 2099609600 | bytes 14746240 | tf_op jit(solution)/shard_map/dot_general | solution.py:337
  149.0 0.7 collective-permute-start.1
  150.1 7.1 %fusion.2 = bf16[160,2560]{1,0:T(8,128)(2,1)S(1)} fusion(bf16[2560,2560]{1,0:T(8,128)(2,1)} %shard_map.59, bf16[160,2560]{1,0:T(8,128)(2,1)S(1)} %get-tuple-element.5, f32[160]{0:T(256)S(1)} %add_rsqrt_fusion.1), kind=kOutput, calls=%fused_computation.5 | convolution fusion | flops 2099609600 | bytes 14746240 | tf_op jit(solution)/shard_map/dot_general | solution.py:337
  157.2 0.8 collective-permute-start.2
  158.4 9.2 %fusion.10 = (f32[160]{0:T(256)S(1)}, f32[160,2560]{1,0:T(8,128)S(1)}) fusion(bf16[160,2560]{1,0:T(8,128)(2,1)S(1)} %get-tuple-element.3, f32[160]{0:T(256)S(1)} %add_rsqrt_fusion, bf16[160,2560]{1,0:T(8,128)(2,1)S(1)} %copy-done.2, bf16[2560,2560]{1,0:T(8,128)(2,1)} %shard_map.59), kind=kOutput, calls=%fused_computation.21 | convolution fusion | flops 2098790272 | bytes 16385280 | tf_op jit(solution)/shard_map/dot_general | solution.py:346
  167.7 0.5 fusion.14
  168.1 0.9 collective-permute-start.3
  169.1 9.2 %fusion.15 = (f32[160]{0:T(256)S(1)}, f32[160,2560]{1,0:T(8,128)S(1)}) fusion(bf16[160,2560]{1,0:T(8,128)(2,1)S(1)} %get-tuple-element.3, f32[160]{0:T(256)S(1)} %add_rsqrt_fusion, bf16[160,2560]{1,0:T(8,128)(2,1)S(1)} %broadcast_select_fusion.3, bf16[2560,2560]{1,0:T(8,128)(2,1)} %shard_map.59), kind=kOutput, calls=%fused_computation.26 | convolution fusion | flops 2098790272 | bytes 16385280 | tf_op jit(solution)/shard_map/dot_general | solution.py:346
  178.8 0.7 collective-permute-start.4
  179.7 9.2 %fusion.20 = (f32[160]{0:T(256)S(1)}, f32[160,2560]{1,0:T(8,128)S(1)}) fusion(bf16[160,2560]{1,0:T(8,128)(2,1)S(1)} %get-tuple-element.3, f32[160]{0:T(256)S(1)} %add_rsqrt_fusion, bf16[160,2560]{1,0:T(8,128)(2,1)S(1)} %broadcast_select_fusion.1, bf16[2560,2560]{1,0:T(8,128)(2,1)} %shard_map.59), kind=kOutput, calls=%fused_computation.31 | convolution fusion | flops 2098790272 | bytes 16385280 | tf_op jit(solution)/shard_map/dot_general | solution.py:346
  188.9 0.5 fusion.24
  189.4 1.3 collective-permute-start.5
  190.9 0.7 convert_reduce_fusion
  191.6 30.0 %collective-permute-done.5 = bf16[160,2560]{1,0:T(8,128)(2,1)S(1)} collective-permute-done((bf16[160,2560]{1,0:T(8,128)(2,1)S(1)}, bf16[160,2560]{1,0:T(8,128)(2,1)S(1)}, u32[]{:S(2)}, u32[]{:S(2)}) %collective-permute-start.5) | collective-permute-done | bytes 819232 | tf_op jit(solution)/shard_map/ppermute | solution.py:351
  221.9 0.6 broadcast_in_dim.12.live_ref
  222.6 50.2 %shard_map.60.own_ref = bf16[160,640]{1,0:T(8,128)(2,1)S(1)} custom-call(bf16[2,160,2560]{2,1,0:T(8,128)(2,1)S(1)} %maximum_select_fusion.sent_ref, f32[8,128]{1,0:T(8,128)S(1)} %broadcast_in_dim.12.live_ref), custom_call_target="tpu_custom_call" | custom-call | tf_op jit(solution)/shard_map/pallas_call | solution.py:257
  272.8 0.7 copy-done.1
  273.4 35.2 %shard_map.61.act_inverse_ref.grad_inverse_ref = bf16[1280,640]{1,0:T(8,128)(2,1)} custom-call(bf16[160,640]{1,0:T(8,128)(2,1)} %copy-done.1), custom_call_target="tpu_custom_call" | custom-call | tf_op jit(solution)/shard_map/pallas_call | solution.py:168
  308.7 1.4 copy-done
  310.1 3.2 %shard_map.62 = (bf16[1,160,2560]{2,1,0:T(8,128)(2,1)}, bf16[1,160,2560]{2,1,0:T(8,128)(2,1)}) custom-call(bf16[160,2560]{1,0:T(8,128)(2,1)S(1)} %get-tuple-element.9.act_ref, bf16[160,2560]{1,0:T(8,128)(2,1)S(1)} %broadcast_select_fusion.grad_ref, bf16[1280,640]{1,0:T(8,128)(2,1)S(1)} %copy-done, bf16[1280,640]{1,0:T(8,128)(2,1)S(1)} %copy-done), custom_call_target="tpu_custom_call" | custom-call | tf_op jit(solution)/shard_map/pallas_call | solution.py:301
  (30 shorter events, 2.6 us)
Async XLA Ops:
  0.6 130.3 %copy-start.3 = (bf16[160,2560]{1,0:T(8,128)(2,1)S(1)}, bf16[160,2560]{1,0:T(8,128)(2,1)}, u32[]{:S(2)}) copy-start(bf16[160,2560]{1,0:T(8,128)(2,1)} %param.4) | copy-start | bytes 2457604
  138.3 3.2 %collective-permute-start = (bf16[160,2560]{1,0:T(8,128)(2,1)S(1)}, bf16[160,2560]{1,0:T(8,128)(2,1)S(1)}, u32[]{:S(2)}, u32[]{:S(2)}) collective-permute-start(bf16[160,2560]{1,0:T(8,128)(2,1)S(1)} %fusion), channel_id=1, source_target_pairs={{0,8},{1,9},{2,10},{3,11},{4,12},{5,13},{6,14},{7,15}} | collective-permute-start | bytes 2457608 | tf_op jit(solution)/shard_map/ppermute | solution.py:339
  149.0 0.7 collective-permute-start.1
  157.2 1.3 copy-start.2
  157.2 0.9 collective-permute-start.2
  168.1 0.9 collective-permute-start.3
  178.8 0.7 collective-permute-start.4
  188.9 1.8 copy-start.4
  189.4 32.2 %collective-permute-start.5 = (bf16[160,2560]{1,0:T(8,128)(2,1)S(1)}, bf16[160,2560]{1,0:T(8,128)(2,1)S(1)}, u32[]{:S(2)}, u32[]{:S(2)}) collective-permute-start(bf16[160,2560]{1,0:T(8,128)(2,1)S(1)} %get-tuple-element.8), channel_id=1, source_target_pairs={{8,0},{9,1},{10,2},{11,3},{12,4},{13,5},{14,6},{15,7}} | collective-permute-start | bytes 2457608 | tf_op jit(solution)/shard_map/ppermute | solution.py:351
  272.8 0.7 copy-start.1
  308.7 1.4 copy-start
